TPU v7x, 256 devices: a whole 4x4x8 slice. The times are simulated.
256 devices in a mesh: section: 2 (over x_lo), dp: 8 (over z), tensor: 16 (over x_hi, y, core).
Axes of the slice: x: 4 (x_hi: 2, x_lo: 2; x = x_hi * 2 + x_lo), y: 4, z: 8, core: 2. Of those that a mesh axis runs over, the one named last changes fastest.
Arguments:
- grads: bfloat16 [2, 8192, 8192], P('section', 'dp', 'tensor')
- groups: int32 [2, 8192], P('section', 'tensor'), may hold values from 0 to 3
- acts: bfloat16 [2, 8192, 14336], P('section', 'dp', 'tensor'), may hold values from -6 to 6
Outputs:
- hessian: float32 [2, 14336, 3584], P('section', ('tensor', 'dp'))
All inputs are finite; a program needn't handle non-finite values.
Results may differ from a plain program's by a relative error of at most 0.0009.
Values may be sent and summed in bfloat16 or wider, within the bound.
No kernel may reach another device: no remote copies, remote signals or barrier semaphores. Data moves between devices by JAX's collectives and lax.ppermute only.
A program may use at most 256 MiB of HBM per device.

v0:
```python
import jax
import jax.numpy as jnp
from jax import lax
from jax.sharding import PartitionSpec as P

D = 8192
GROUPS = 4
MICRO = 4


def from_behind(value, axis, steps):
    count = lax.axis_size(axis)
    initial, last = (max(0, -steps), min(count, count - steps))
    return lax.ppermute(value, axis, [(source, source + steps) for source in range(initial, last)])


def contract_tokens(left, right):
    return lax.dot_general(
        left, right, (((0,), (0,)), ((), ())), preferred_element_type=jnp.float32
    )


def scale_inputs(weight, cols):
    scaled = (weight[:, :, None] * cols[:, None, :]).astype(jnp.bfloat16)
    return scaled.reshape(cols.shape[0], weight.shape[1] * cols.shape[1])


def on_device(grads, groups, acts):
    onehot = (groups[0][:, None] == jnp.arange(GROUPS, dtype=jnp.int32)[None, :]).astype(
        jnp.float32
    )
    tok_count = grads.shape[1]
    step_rows = tok_count // MICRO
    summed_list = []
    for index in range(MICRO):
        piece = grads[0, index * step_rows : (index + 1) * step_rows]
        later = from_behind(piece, "section", -1)
        total = piece.astype(jnp.float32) + later.astype(jnp.float32)
        partial_value = jnp.dot(total * total, onehot, precision=lax.Precision.HIGHEST)
        summed_list.append(lax.psum(partial_value, "tensor"))
    weight = jnp.concatenate(summed_list, 0)
    weight = weight / D
    block_cols = acts[0]
    factor = 1.0 / (tok_count * lax.axis_size("dp"))
    scaled = scale_inputs(weight, block_cols)
    result = lax.psum_scatter(
        contract_tokens(block_cols, scaled), "dp", scatter_dimension=0, tiled=True
    )
    return (result * factor)[None]


def solution(mesh):
    return jax.shard_map(
        on_device,
        mesh=mesh,
        in_specs=(
            P("section", "dp", "tensor"),
            P("section", "tensor"),
            P("section", "dp", "tensor"),
        ),
        out_specs=P("section", ("tensor", "dp"), None),
        check_vma=False,
    )
```

profile of v0, /device:TPU:8, one launch (start us, length us, event | category | flops | bytes accessed | tf_op | source)
XLA Modules:
  0.0 290.2 jit_solution(7216837148318259502)
XLA Ops:
  6.5 0.0 copy-start.1
  6.5 0.0 copy-start.2
  6.5 0.0 reduce-scatter.4.cloned.1.call-start
  6.5 1.3 slice_bitcast_fusion.3
  7.9 1.3 collective-permute-start
  9.2 1.3 collective-permute-start.1
  10.5 1.3 collective-permute-start.3
  11.8 1.3 collective-permute-start.2
  13.1 3.5 %bitcast_convert_fusion = f32[1024,896]{1,0:T(8,128)} fusion(bf16[1,1024,896]{2,1,0:T(8,128)(2,1)} %param.5), kind=kLoop, calls=%fused_computation.3 | loop fusion | flops 917504 | bytes 5505024 | tf_op jit(solution)/shard_map/convert_element_type | solution.py:24
  16.6 2.4 collective-permute-done
  19.0 0.0 copy-done.1
  19.0 0.0 copy-done.2
  19.0 0.5 fusion.16
  19.4 5.2 %collective-permute-done.1 = bf16[256,512]{1,0:T(8,128)(2,1)S(1)} collective-permute-done((bf16[256,512]{1,0:T(8,128)(2,1)S(1)}, bf16[256,512]{1,0:T(8,128)(2,1)S(1)}, u32[]{:S(2)}, u32[]{:S(2)}) %collective-permute-start.1) | collective-permute-done | bytes 262176 | tf_op jit(solution)/shard_map/ppermute | solution.py:14
  24.6 0.5 fusion.11
  25.0 5.2 %collective-permute-done.3 = bf16[256,512]{1,0:T(8,128)(2,1)S(1)} collective-permute-done((bf16[256,512]{1,0:T(8,128)(2,1)S(1)}, bf16[256,512]{1,0:T(8,128)(2,1)S(1)}, u32[]{:S(2)}, u32[]{:S(2)}) %collective-permute-start.3) | collective-permute-done | bytes 262176 | tf_op jit(solution)/shard_map/ppermute | solution.py:14
  30.2 0.5 fusion.1
  30.7 4.0 %collective-permute-done.2 = bf16[256,512]{1,0:T(8,128)(2,1)S(1)} collective-permute-done((bf16[256,512]{1,0:T(8,128)(2,1)S(1)}, bf16[256,512]{1,0:T(8,128)(2,1)S(1)}, u32[]{:S(2)}, u32[]{:S(2)}) %collective-permute-start.2) | collective-permute-done | bytes 262176 | tf_op jit(solution)/shard_map/ppermute | solution.py:14
  34.7 0.5 fusion.6
  35.1 63.4 %all-reduce = (f32[256,4]{0,1:T(4,128)S(1)}, f32[256,4]{0,1:T(4,128)S(1)}, f32[256,4]{0,1:T(4,128)S(1)}, f32[256,4]{0,1:T(4,128)S(1)}) all-reduce(f32[256,4]{0,1:T(4,128)S(1)} %fusion.1, f32[256,4]{0,1:T(4,128)S(1)} %fusion.6, f32[256,4]{0,1:T(4,128)S(1)} %fusion.11, ...), channel_id=1, replica_groups=mesh['section'=2,'dp'=8,'tensor'=16] {'tensor'}, use_global_device_ids=true, to_apply=%region_3.0 | all-reduce | flops 4096 | bytes 32768 | tf_op jit(solution)/shard_map/psum | solution.py:40
  98.6 0.2 copy.6
  98.8 7.3 %multiply_convert_fusion = bf16[1024,4,896]{2,1,0:T(4,128)(2,1)S(1)} fusion(f32[1024,896]{1,0:T(8,128)} %bitcast_convert_fusion, f32[1024,4]{1,0:T(8,128)S(1)} %copy.6), kind=kLoop, calls=%fused_computation | loop fusion | flops 7340032 | bytes 11026432 | tf_op jit(solution)/shard_map/convert_element_type | solution.py:24
  106.1 0.0 copy-start
  106.1 4.2 %copy.10 = bf16[128,8,4,896]{3,1,2,0:T(8,128)(2,1)} copy(bf16[128,8,4,896]{3,2,1,0:T(4,128)(2,1)S(1)} %bitcast.33) | data formatting | bytes 14680064
  110.3 0.0 copy-done
  110.3 12.7 %convolution_bitcast_fusion = f32[896,3584]{0,1:T(8,128)} fusion(bf16[1024,3584]{1,0:T(8,128)(2,1)} %bitcast.34, bf16[1,1024,896]{2,1,0:T(8,128)(2,1)S(1)} %copy-done), kind=kOutput, calls=%fused_computation.1 | convolution fusion | flops 6576668672 | bytes 22020096 | tf_op jit(solution)/shard_map/dot_general | solution.py:18
  123.0 14.2 %copy.8 = f32[896,3584]{1,0:T(8,128)} copy(f32[896,3584]{0,1:T(8,128)} %convolution_bitcast_fusion) | data formatting | bytes 25690112
  137.2 0.0 reduce-scatter.4.cloned.1.call-update
  137.2 140.4 %reduce-scatter.4.cloned.1.call-done = f32[112,3584]{1,0:T(8,128)} async-done(((f32[896,3584]{1,0:T(8,128)}), f32[112,3584]{1,0:T(8,128)}) %reduce-scatter.4.cloned.1.call-update) | async-done | bytes 1605648
  277.5 1.8 copy.9
  279.3 1.4 multiply_bitcast_fusion
  280.7 2.7 copy.7
  (1 shorter events, 0.0 us)
Async XLA Ops:
  6.5 12.4 %copy-start.1 = (bf16[1,1024,512]{2,1,0:T(8,128)(2,1)S(1)}, bf16[1,1024,512]{2,1,0:T(8,128)(2,1)}, u32[]{:S(2)}) copy-start(bf16[1,1024,512]{2,1,0:T(8,128)(2,1)} %param.3) | copy-start | bytes 3145732
  6.5 12.4 %copy-start.2 = (s32[1,512]{1,0:T(1,128)S(1)}, s32[1,512]{1,0:T(1,128)}, u32[]{:S(2)}) copy-start(s32[1,512]{1,0:T(1,128)} %param.4) | copy-start | bytes 6148
  6.5 271.0 %reduce-scatter.4.cloned.1.call-start = ((), (), s32[]{:S(2)}) async-start(), calls=%async_computation.1 | async-start | bytes 14450688
  7.9 11.1 %collective-permute-start = (bf16[256,512]{1,0:T(8,128)(2,1)S(1)}, bf16[256,512]{1,0:T(8,128)(2,1)S(1)}, u32[]{:S(2)}, u32[]{:S(2)}) collective-permute-start(bf16[256,512]{1,0:T(8,128)(2,1)S(1)} %get-tuple-element.9), channel_id=1, source_target_pairs={{128,0},{129,1},{130,2},{131,3},{132,4},{133,5},{134,6},{135,7},{1... | collective-permute-start | bytes 786440 | tf_op jit(solution)/shard_map/ppermute | solution.py:14
  9.2 15.4 %collective-permute-start.1 = (bf16[256,512]{1,0:T(8,128)(2,1)S(1)}, bf16[256,512]{1,0:T(8,128)(2,1)S(1)}, u32[]{:S(2)}, u32[]{:S(2)}) collective-permute-start(bf16[256,512]{1,0:T(8,128)(2,1)S(1)} %get-tuple-element.10), channel_id=1, source_target_pairs={{128,0},{129,1},{130,2},{131,3},{132,4},{133,5},{134,6},{135,7},{1... | collective-permute-start | bytes 786440 | tf_op jit(solution)/shard_map/ppermute | solution.py:14
  10.5 19.7 %collective-permute-start.3 = (bf16[256,512]{1,0:T(8,128)(2,1)S(1)}, bf16[256,512]{1,0:T(8,128)(2,1)S(1)}, u32[]{:S(2)}, u32[]{:S(2)}) collective-permute-start(bf16[256,512]{1,0:T(8,128)(2,1)S(1)} %get-tuple-element.11), channel_id=1, source_target_pairs={{128,0},{129,1},{130,2},{131,3},{132,4},{133,5},{134,6},{135,7},{1... | collective-permute-start | bytes 786440 | tf_op jit(solution)/shard_map/ppermute | solution.py:14
  11.8 22.9 %collective-permute-start.2 = (bf16[256,512]{1,0:T(8,128)(2,1)S(1)}, bf16[256,512]{1,0:T(8,128)(2,1)S(1)}, u32[]{:S(2)}, u32[]{:S(2)}) collective-permute-start(bf16[256,512]{1,0:T(8,128)(2,1)S(1)} %get-tuple-element.12), channel_id=1, source_target_pairs={{128,0},{129,1},{130,2},{131,3},{132,4},{133,5},{134,6},{135,7},{1... | collective-permute-start | bytes 786440 | tf_op jit(solution)/shard_map/ppermute | solution.py:14
  106.1 4.2 %copy-start = (bf16[1,1024,896]{2,1,0:T(8,128)(2,1)S(1)}, bf16[1,1024,896]{2,1,0:T(8,128)(2,1)}, u32[]{:S(2)}) copy-start(bf16[1,1024,896]{2,1,0:T(8,128)(2,1)} %param.5) | copy-start | bytes 5505028
Sparse Core Ops, SparseCore 0:
  137.3 140.1 reduce-scatter.3
where the time goes:
time: 292 us; the launch traced here: 290 us
  waiting for transfers between devices  157 us (54%)
  blocking collectives  63.4 us (22%)
  local copies, waits for them, and re-layouts  24.4 us (8%)
  matrix products  14.5 us (5%)
  between operations  13.5 us (5%)
  other arithmetic  12.2 us (4%)
  starting transfers between devices  5.17 us (2%)
    unnamed x2, waiting for transfers between devices  140 us
    psum x1, blocking collectives, on_device(): summed_list.append(lax.psum(partial_value, 'tensor'))  63.4 us
    unnamed x9, local copies, waits for them, and re-layouts  20.1 us
    ppermute x4, waiting for transfers between devices, from_behind(): lax.ppermute(value, axis, [(source, source + steps) for source in range(i...  16.7 us
    dot_general x1, matrix products, contract_tokens(): lax.dot_general(left, right, (((0,), (0,)), ((), ())), preferred_element_...  12.7 us
    convert_element_type x2, other arithmetic, scale_inputs(): scaled = (weight[:, :, None] * cols[:, None, :]).astype(jnp.bfloat16)  10.8 us
  transfers between devices with their start and end apart: 5, of which 5 were waited for; matrix products, arithmetic and copies ran while one was open for 2% of the time, Pallas kernels for 0%

commit v1 on v0

v1 whole, which is shorter than its diff:
```python
import jax
import jax.numpy as jnp
from jax import lax
from jax.experimental import pallas as pl
from jax.experimental.pallas import tpu as pltpu
from jax.sharding import PartitionSpec as P

D = 8192
GROUPS = 4
MICRO = 4
DP = 8
SENT = jnp.float16
VMEM_LIMIT = 48 * 1024 * 1024


def shift(value, axis, steps):
    count = lax.axis_size(axis)
    return lax.ppermute(value, axis, [(i, (i + steps) % count) for i in range(count)])


def square_kernel(groups_ref, own_ref, other_ref, out_ref):
    group = lax.broadcasted_iota(jnp.int32, (16, groups_ref.shape[1]), 0)
    onehot = jnp.where(groups_ref[...] == group, 1.0, 0.0).astype(jnp.bfloat16)
    total = own_ref[...].astype(jnp.float32) + other_ref[...].astype(jnp.float32)
    rest = total * total
    result = jnp.zeros((16, own_ref.shape[0]), jnp.float32)
    for _ in range(3):
        part = rest.astype(jnp.bfloat16)
        rest = rest - part.astype(jnp.float32)
        result += lax.dot_general(
            onehot, part, (((1,), (1,)), ((), ())), preferred_element_type=jnp.float32
        )
    out_ref[...] = result[:8]


def group_squares(groups, own, other):
    return pl.pallas_call(
        square_kernel,
        out_shape=jax.ShapeDtypeStruct((8, own.shape[0]), jnp.float32),
        compiler_params=pltpu.CompilerParams(vmem_limit_bytes=VMEM_LIMIT),
    )(groups, own, other)


def scale_kernel(weight_ref, acts_ref, rows_ref, scaled_ref, product_ref):
    width = acts_ref.shape[1]
    acts = acts_ref[...].astype(jnp.float32)

    @pl.when(pl.program_id(0) == 0)
    def _():
        product_ref[...] = jnp.zeros_like(product_ref)

    for g in range(GROUPS):
        cols = slice(g * width, (g + 1) * width)
        scaled = (weight_ref[:, g : g + 1] * acts).astype(jnp.bfloat16)
        scaled_ref[:, cols] = scaled
        product_ref[:, cols] += jnp.dot(rows_ref[...], scaled, preferred_element_type=jnp.float32)


def scale_and_first(weight, acts, rows):
    tokens, width = acts.shape
    block = 256
    return pl.pallas_call(
        scale_kernel,
        grid=(tokens // block,),
        in_specs=[
            pl.BlockSpec((block, GROUPS), lambda k: (k, 0)),
            pl.BlockSpec((block, width), lambda k: (k, 0)),
            pl.BlockSpec((rows.shape[0], block), lambda k: (0, k)),
        ],
        out_specs=[
            pl.BlockSpec((block, GROUPS * width), lambda k: (k, 0)),
            pl.BlockSpec((rows.shape[0], GROUPS * width), lambda k: (0, 0)),
        ],
        out_shape=[
            jax.ShapeDtypeStruct((tokens, GROUPS * width), jnp.bfloat16),
            jax.ShapeDtypeStruct((rows.shape[0], GROUPS * width), jnp.float32),
        ],
        compiler_params=pltpu.CompilerParams(vmem_limit_bytes=VMEM_LIMIT),
    )(weight, acts, rows)


def product_kernel(rows_ref, scaled_ref, out_ref):
    out_ref[...] = jnp.dot(rows_ref[...], scaled_ref[...], preferred_element_type=jnp.float32)


def product(rows, scaled):
    tokens, cols = scaled.shape
    count = rows.shape[0]
    block = cols // GROUPS
    return pl.pallas_call(
        product_kernel,
        grid=(GROUPS,),
        in_specs=[
            pl.BlockSpec((count, tokens), lambda g: (0, 0)),
            pl.BlockSpec((tokens, block), lambda g: (0, g)),
        ],
        out_specs=pl.BlockSpec((count, block), lambda g: (0, g)),
        out_shape=jax.ShapeDtypeStruct((count, cols), jnp.float32),
        compiler_params=pltpu.CompilerParams(vmem_limit_bytes=VMEM_LIMIT),
        cost_estimate=pl.CostEstimate(
            flops=2 * count * tokens * cols,
            bytes_accessed=2 * tokens * cols + 4 * count * cols,
            transcendentals=0,
        ),
    )(rows, scaled)


def on_device(grads, groups, acts):
    me = lax.axis_index("dp")
    own = grads[0]
    tokens = own.shape[0]
    step = tokens // MICRO

    partial = []
    for index in range(MICRO):
        piece = own[index * step : (index + 1) * step]
        later = lax.ppermute(piece, "section", [(1, 0)])
        partial.append(group_squares(groups, piece, later)[:GROUPS])
    partial = jnp.concatenate(partial, 1)
    count = lax.axis_size("tensor")
    spread = jnp.broadcast_to(partial[None], (count, GROUPS, tokens))
    weight = lax.all_to_all(spread, "tensor", 0, 0, tiled=True).sum(0) / D

    cols = acts[0]
    width = cols.shape[1]
    rows = width // DP
    turned = cols.T
    peak = jnp.max(jnp.abs(turned), axis=0).astype(jnp.float32)
    blocks = [
        lax.dynamic_slice_in_dim(turned, ((me + k) % DP) * rows, rows, 0) for k in range(DP)
    ]

    top = jnp.maximum(jnp.max(weight * (peak * peak)[None]), 1e-30)
    top = jnp.broadcast_to(top, (8, 128))
    top_left, top_right = shift(top, "dp", 1), shift(top, "dp", -1)
    near = jnp.maximum(top, jnp.maximum(top_left, top_right))
    every = jnp.maximum(near, jnp.maximum(shift(near, "dp", 3), shift(near, "dp", -3)))
    own_scale = (32768.0 / tokens) / top[0, 0]
    left_back = (tokens / 32768.0) * top_left[0, 0]
    right_back = (tokens / 32768.0) * top_right[0, 0]
    all_scale = (32768.0 / (tokens * DP)) / every[0, 0]
    all_back = (tokens * DP / 32768.0) * every[0, 0]

    scaled, far = scale_and_first(weight.T, cols, blocks[4])
    third = product(jnp.concatenate([blocks[3], blocks[5]], 0), scaled)
    second = product(jnp.concatenate([blocks[2], blocks[6]], 0), scaled)
    first = product(jnp.concatenate([blocks[1], blocks[7]], 0), scaled)
    mine = product(blocks[0], scaled)

    half = GROUPS * width // 2
    a, b = slice(0, half), slice(half, 2 * half)
    up, down = slice(0, rows), slice(rows, 2 * rows)

    def pack(value, scale):
        return (value * scale).astype(SENT)

    def unpack(value, back):
        return value.astype(jnp.float32) * back

    def send(value, steps):
        return shift(value, "dp", steps)

    r1 = send(pack(far[:, a], own_scale), 1)
    l1 = send(pack(far[:, b], own_scale), -1)
    r2 = send(pack(third[up, b], own_scale), 1)
    l2 = send(pack(third[down, a], own_scale), -1)
    r3 = send(pack(third[up, a] + unpack(r1, left_back), all_scale), 1)
    l3 = send(pack(third[down, b] + unpack(l1, right_back), all_scale), -1)
    r4 = send(pack(second[up, b] + unpack(r2, left_back), all_scale), 1)
    l4 = send(pack(second[down, a] + unpack(l2, right_back), all_scale), -1)
    r5 = send(pack(second[up, a] + unpack(r3, all_back), all_scale), 1)
    l5 = send(pack(second[down, b] + unpack(l3, all_back), all_scale), -1)
    r6 = send(pack(first[up, b] + unpack(r4, all_back), all_scale), 1)
    l6 = send(pack(first[down, a] + unpack(l4, all_back), all_scale), -1)
    r7 = send(pack(first[up, a] + unpack(r5, all_back), all_scale), 1)
    l7 = send(pack(first[down, b] + unpack(l5, all_back), all_scale), -1)

    factor = 1.0 / (tokens * DP)
    left = mine[:, a] + (unpack(r7, all_back) + unpack(l6, all_back))
    right = mine[:, b] + (unpack(r6, all_back) + unpack(l7, all_back))
    return (jnp.concatenate([left, right], 1) * factor)[None]


def solution(mesh):
    return jax.shard_map(
        on_device,
        mesh=mesh,
        in_specs=(
            P("section", "dp", "tensor"),
            P("section", "tensor"),
            P("section", "dp", "tensor"),
        ),
        out_specs=P("section", ("tensor", "dp"), None),
        check_vma=False,
    )
```

time: 292 us -> 141 us (0.48)
  waiting for transfers between devices: 157 us -> 41.6 us
  blocking collectives: 63.4 us -> 0 us
  starting transfers between devices: 5.17 us -> 43.9 us
  Pallas kernels: 0 us -> 28 us
  matrix products: 14.5 us -> 0 us
  local copies, waits for them, and re-layouts: 24.4 us -> 12.2 us
  between operations: 13.5 us -> 3.68 us
    unnamed x2 -> x0, waiting for transfers between devices: 140 us -> none
    psum x1 -> x0, blocking collectives: 63.4 us -> none  [on_device(): summed_list.append(lax.psum(partial_value, 'tensor'))]
    ppermute x4 -> x22, starting transfers between devices: 5.17 us -> 36.5 us  [the longest x18 31.4 us: shift(): lax.ppermute(value, axis, [(i, (i + steps) % count) for i in range(count)])]
    pallas_call x0 -> x9, Pallas kernels: none -> 28 us  [the longest x4 20.3 us: product(): pl.pallas_call(product_kernel, grid=(GROUPS,), in_specs=[pl.BlockSpec((co...]
    ppermute x4 -> x22, waiting for transfers between devices: 16.7 us -> 36.8 us  [the longest x18 24.4 us: shift(): lax.ppermute(value, axis, [(i, (i + steps) % count) for i in range(count)])]
    unnamed x9 -> x16, local copies, waits for them, and re-layouts: 20.1 us -> 0.78 us
    dot_general x5 -> x0, matrix products: 14.5 us -> none  [the longest x1 12.7 us: contract_tokens(): lax.dot_general(left, right, (((0,), (0,)), ((), ())), preferred_element_...]
    another operation x0 -> x9, local copies, waits for them, and re-layouts: none -> 7.44 us
  transfers between devices with their start and end apart: 5 -> 23, of which waited for: 5 -> 12; matrix products, arithmetic and copies ran while one was open for 2% -> 8% of each run, Pallas kernels for 0% -> 20%
where the time goes in v1:
time: 141 us
  starting transfers between devices  43.9 us (31%)
  waiting for transfers between devices  41.6 us (30%)
  Pallas kernels  28 us (20%)
  local copies, waits for them, and re-layouts  12.2 us (9%)
  other arithmetic  11.3 us (8%)
  between operations  3.68 us (3%)
    ppermute x18, starting transfers between devices, shift(): lax.ppermute(value, axis, [(i, (i + steps) % count) for i in range(count)])  31.4 us
    ppermute x18, waiting for transfers between devices, shift(): lax.ppermute(value, axis, [(i, (i + steps) % count) for i in range(count)])  24.4 us
    pallas_call x4, Pallas kernels, product(): pl.pallas_call(product_kernel, grid=(GROUPS,), in_specs=[pl.BlockSpec((co...  20.3 us
    ppermute x4, waiting for transfers between devices, on_device(): later = lax.ppermute(piece, 'section', [(1, 0)])  12.4 us
    another operation x9, local copies, waits for them, and re-layouts  7.44 us
    all_to_all x1, starting transfers between devices, on_device(): weight = lax.all_to_all(spread, 'tensor', 0, 0, tiled=True).sum(0) / D  7.39 us
    convert_element_type x4, other arithmetic, pack(): return (value * scale).astype(SENT)  6.31 us
    ppermute x4, starting transfers between devices, on_device(): later = lax.ppermute(piece, 'section', [(1, 0)])  5.17 us
  transfers between devices with their start and end apart: 23, of which 12 were waited for; matrix products, arithmetic and copies ran while one was open for 8% of the time, Pallas kernels for 20%

profile of v1, /device:TPU:8, one launch (start us, length us, event | category | flops | bytes accessed | tf_op | source)
XLA Modules:
  0.0 140.7 jit_solution(12043804401053488088)
XLA Ops:
  6.7 2.1 %constant_dynamic-slice_fusion.1 = (bf16[1,1024,112]{2,1,0:T(8,128)(2,1)}, bf16[1,1024,112]{2,1,0:T(8,128)(2,1)}, bf16[1,1024,112]{2,1,0:T(8,128)(2,1)}, bf16[1,...) fusion(bf16[1,1024,896]{2,1,0:T(8,128)(2,1)S(1)} %copy-done, ...), kind=kLoop, calls=%fused_computation.56 | loop fusion | bytes 3670048 | tf_op jit(solution)/shard_map/dynamic-slice.14
  8.8 1.8 %copy.41 = bf16[1,1024,112]{1,2,0:T(8,128)(2,1)} copy(bf16[1,1024,112]{2,1,0:T(8,128)(2,1)} %get-tuple-element.21) | data formatting | bytes 458752 | tf_op jit(solution)/shard_map/dynamic-slice.14
  10.6 1.8 %copy.42 = bf16[1,1024,112]{1,2,0:T(8,128)(2,1)} copy(bf16[1,1024,112]{2,1,0:T(8,128)(2,1)} %get-tuple-element.28) | data formatting | bytes 458752 | tf_op jit(solution)/shard_map/dynamic-slice.15
  14.1 4.1 %collective-permute-done.1.other_ref = bf16[256,512]{1,0:T(8,128)(2,1)} collective-permute-done((bf16[256,512]{1,0:T(8,128)(2,1)S(1)}, bf16[256,512]{1,0:T(8,128)(2,1)}, u32[]{:S(2)}, u32[]{:S(2)}) %collective-permute-start.1) | collective-permute-done | bytes 262176 | tf_op jit(solution)/shard_map/ppermute | solution.py:117
  19.5 4.2 %collective-permute-done.2.other_ref = bf16[256,512]{1,0:T(8,128)(2,1)S(1)} collective-permute-done((bf16[256,512]{1,0:T(8,128)(2,1)S(1)}, bf16[256,512]{1,0:T(8,128)(2,1)S(1)}, u32[]{:S(2)}, u32[]{:S(2)}) %collective-permute-start.2) | collective-permute-done | bytes 262176 | tf_op jit(solution)/shard_map/ppermute | solution.py:117
  24.1 4.1 %collective-permute-done.3.other_ref = bf16[256,512]{1,0:T(8,128)(2,1)S(1)} collective-permute-done((bf16[256,512]{1,0:T(8,128)(2,1)S(1)}, bf16[256,512]{1,0:T(8,128)(2,1)S(1)}, u32[]{:S(2)}, u32[]{:S(2)}) %collective-permute-start.3) | collective-permute-done | bytes 262176 | tf_op jit(solution)/shard_map/ppermute | solution.py:117
  29.3 7.4 %all-to-all-start = ((f32[16,4,1024]{2,1,0:T(4,128)}), f32[16,4,1024]{2,1,0:T(4,128)S(1)}, u32[]{:S(2)}, u32[]{:S(2)}) async-start(f32[16,4,1024]{2,1,0:T(4,128)} %broadcast_in_dim.4), calls=%async_computation | async-start | bytes 524288 | tf_op jit(solution)/shard_map/all_to_all | solution.py:122
  38.9 4.8 %all-to-all-done = f32[16,4,1024]{2,1,0:T(4,128)S(1)} async-done(((f32[16,4,1024]{2,1,0:T(4,128)}), f32[16,4,1024]{2,1,0:T(4,128)S(1)}, u32[]{:S(2)}, u32[]{:S(2)}) %all-to-all-start) | async-done | bytes 262176 | tf_op jit(solution)/shard_map/all_to_all | solution.py:122
  45.0 2.0 %collective-permute-start.5 = (f32[8,128]{1,0:T(8,128)S(1)}, f32[8,128]{1,0:T(8,128)S(1)}, u32[]{:S(2)}, u32[]{:S(2)}) collective-permute-start(f32[8,128]{1,0:T(8,128)S(1)} %broadcast_in_dim.5), channel_id=1, source_target_pairs={{0,16},{16,32},{32,48},{48,64},{64,80},{80,96},{96,112},{112,0},{1... | collective-permute-start | bytes 12296 | tf_op jit(solution)/shard_map/ppermute | solution.py:18
  47.0 4.0 %collective-permute-start.6 = (f32[8,128]{1,0:T(8,128)S(1)}, f32[8,128]{1,0:T(8,128)S(1)}, u32[]{:S(2)}, u32[]{:S(2)}) collective-permute-start(f32[8,128]{1,0:T(8,128)S(1)} %broadcast_in_dim.5), channel_id=1, source_target_pairs={{0,112},{16,0},{32,16},{48,32},{64,48},{80,64},{96,80},{112,96},{1... | collective-permute-start | bytes 12296 | tf_op jit(solution)/shard_map/ppermute | solution.py:18
  51.3 4.4 %shard_map.41 = (bf16[1024,3584]{1,0:T(8,128)(2,1)}, f32[112,3584]{1,0:T(8,128)S(1)}) custom-call(f32[1024,4]{1,0:T(8,128)S(1)} %bitcast.44, bf16[1024,896]{1,0:T(8,128)(2,1)S(1)} %bitcast.43, bf16[112,1024]{1,0:T(8,128)(2,1)S(1)} %bitcast.45), custom_call_target="tpu_custom_call" | custom-call | tf_op jit(solution)/shard_map/pallas_call | solution.py:62
  55.8 2.0 %collective-permute-start.18 = (f16[112,1792]{1,0:T(8,128)(2,1)S(1)}, f16[112,1792]{1,0:T(8,128)(2,1)S(1)}, u32[]{:S(2)}, u32[]{:S(2)}) collective-permute-start(f16[112,1792]{1,0:T(8,128)(2,1)S(1)} %get-tuple-element.32), channel_id=1, source_target_pairs={{0,112},{16,0},{32,16},{48,32},{64,48},{80,64},{96,80},{112,96},{1... | collective-permute-start | bytes 1204232 | tf_op jit(solution)/shard_map/ppermute | solution.py:18
  57.9 3.2 %collective-permute-start.7 = (f32[8,128]{1,0:T(8,128)S(1)}, f32[8,128]{1,0:T(8,128)S(1)}, u32[]{:S(2)}, u32[]{:S(2)}) collective-permute-start(f32[8,128]{1,0:T(8,128)S(1)} %maximum_maximum_fusion.1), channel_id=1, source_target_pairs={{0,48},{16,64},{32,80},{48,96},{64,112},{80,0},{96,16},{112,32},{1... | collective-permute-start | bytes 12296 | tf_op jit(solution)/shard_map/ppermute | solution.py:18
  61.1 1.9 %collective-permute-start.8 = (f32[8,128]{1,0:T(8,128)S(1)}, f32[8,128]{1,0:T(8,128)S(1)}, u32[]{:S(2)}, u32[]{:S(2)}) collective-permute-start(f32[8,128]{1,0:T(8,128)S(1)} %maximum_maximum_fusion.1), channel_id=1, source_target_pairs={{0,80},{16,96},{32,112},{48,0},{64,16},{80,32},{96,48},{112,64},{1... | collective-permute-start | bytes 12296 | tf_op jit(solution)/shard_map/ppermute | solution.py:18
  63.1 5.2 %shard_map.45 = f32[224,3584]{1,0:T(8,128)S(1)} custom-call(bf16[224,1024]{1,0:T(8,128)(2,1)S(1)} %pad_maximum_fusion.2.rows_ref, bf16[1024,3584]{1,0:T(8,128)(2,1)} %get-tuple-element.7.scaled_ref), custom_call_target="tpu_custom_call" | custom-call | flops 1644167168 | bytes 10551296 | tf_op jit(solution)/shard_map/pallas_call | solution.py:90
  73.1 1.9 %collective-permute-start.12 = (f16[112,1792]{1,0:T(8,128)(2,1)}, f16[112,1792]{1,0:T(8,128)(2,1)S(1)}, u32[]{:S(2)}, u32[]{:S(2)}) collective-permute-start(f16[112,1792]{1,0:T(8,128)(2,1)} %get-tuple-element.20), channel_id=1, source_target_pairs={{0,112},{16,0},{32,16},{48,32},{64,48},{80,64},{96,80},{112,96},{1... | collective-permute-start | bytes 1204232 | tf_op jit(solution)/shard_map/ppermute | solution.py:18
  75.1 3.1 %collective-permute-start.19 = (f16[112,1792]{1,0:T(8,128)(2,1)S(1)}, f16[112,1792]{1,0:T(8,128)(2,1)S(1)}, u32[]{:S(2)}, u32[]{:S(2)}) collective-permute-start(f16[112,1792]{1,0:T(8,128)(2,1)S(1)} %get-tuple-element.18), channel_id=1, source_target_pairs={{0,112},{16,0},{32,16},{48,32},{64,48},{80,64},{96,80},{112,96},{1... | collective-permute-start | bytes 1204232 | tf_op jit(solution)/shard_map/ppermute | solution.py:18
  78.6 5.2 %shard_map.44 = f32[224,3584]{1,0:T(8,128)S(1)} custom-call(bf16[224,1024]{1,0:T(8,128)(2,1)S(1)} %pad_maximum_fusion.1.rows_ref, bf16[1024,3584]{1,0:T(8,128)(2,1)} %get-tuple-element.7.scaled_ref), custom_call_target="tpu_custom_call" | custom-call | flops 1644167168 | bytes 10551296 | tf_op jit(solution)/shard_map/pallas_call | solution.py:90
  85.5 2.9 %collective-permute-done.15 = f16[112,1792]{1,0:T(8,128)(2,1)S(1)} collective-permute-done((f16[112,1792]{1,0:T(8,128)(2,1)S(1)}, f16[112,1792]{1,0:T(8,128)(2,1)S(1)}, u32[]{:S(2)}, u32[]{:S(2)}) %collective-permute-start.15) | collective-permute-done | bytes 401440 | tf_op jit(solution)/shard_map/ppermute | solution.py:18
  88.5 4.0 %collective-permute-done.19 = f16[112,1792]{1,0:T(8,128)(2,1)S(1)} collective-permute-done((f16[112,1792]{1,0:T(8,128)(2,1)S(1)}, f16[112,1792]{1,0:T(8,128)(2,1)S(1)}, u32[]{:S(2)}, u32[]{:S(2)}) %collective-permute-start.19) | collective-permute-done | bytes 401440 | tf_op jit(solution)/shard_map/ppermute | solution.py:18
  92.5 2.5 %collective-permute-done.9 = f16[112,1792]{1,0:T(8,128)(2,1)} collective-permute-done((f16[112,1792]{1,0:T(8,128)(2,1)S(1)}, f16[112,1792]{1,0:T(8,128)(2,1)}, u32[]{:S(2)}, u32[]{:S(2)}) %collective-permute-start.9) | collective-permute-done | bytes 401440 | tf_op jit(solution)/shard_map/ppermute | solution.py:18
  95.0 2.4 %fusion.20 = (f16[112,1792]{1,0:T(8,128)(2,1)}, f16[112,1792]{1,0:T(8,128)(2,1)S(1)}, f16[112,1792]{1,0:T(8,128)(2,1)S(1)}, f16[112,1792]{1,0:T(8,128)(2,1)S(1)}) fusion(f32[224,3584]{1,0:T(8,128)S(1)} %shard_map.44, f16[112,1792]{1,0:T(8,128)(2,1)} %collective-permute-done.9, f32[]{:T(128)} %bitcast.24, f32[]{:T(128)} %bitcast.23, ...), kind=kLoop, calls=%fused_computation.34 | loop fusion | flops 4014080 | bytes 6422544 | tf_op jit(solution)/shard_map/convert_element_type | solution.py:155
  97.3 3.2 %collective-permute-start.13 = (f16[112,1792]{1,0:T(8,128)(2,1)S(1)}, f16[112,1792]{1,0:T(8,128)(2,1)S(1)}, u32[]{:S(2)}, u32[]{:S(2)}) collective-permute-start(f16[112,1792]{1,0:T(8,128)(2,1)S(1)} %get-tuple-element.16), channel_id=1, source_target_pairs={{0,112},{16,0},{32,16},{48,32},{64,48},{80,64},{96,80},{112,96},{1... | collective-permute-start | bytes 1204232 | tf_op jit(solution)/shard_map/ppermute | solution.py:18
  100.6 3.2 %collective-permute-start.20 = (f16[112,1792]{1,0:T(8,128)(2,1)S(1)}, f16[112,1792]{1,0:T(8,128)(2,1)}, u32[]{:S(2)}, u32[]{:S(2)}) collective-permute-start(f16[112,1792]{1,0:T(8,128)(2,1)S(1)} %get-tuple-element.14), channel_id=1, source_target_pairs={{0,112},{16,0},{32,16},{48,32},{64,48},{80,64},{96,80},{112,96},{1... | collective-permute-start | bytes 1204232 | tf_op jit(solution)/shard_map/ppermute | solution.py:18
  104.1 5.2 %shard_map.43 = f32[224,3584]{1,0:T(8,128)S(1)} custom-call(bf16[224,1024]{1,0:T(8,128)(2,1)S(1)} %pad_maximum_fusion.rows_ref, bf16[1024,3584]{1,0:T(8,128)(2,1)} %get-tuple-element.7.scaled_ref), custom_call_target="tpu_custom_call" | custom-call | flops 1644167168 | bytes 10551296 | tf_op jit(solution)/shard_map/pallas_call | solution.py:90
  111.0 5.4 %collective-permute-done.16 = f16[112,1792]{1,0:T(8,128)(2,1)S(1)} collective-permute-done((f16[112,1792]{1,0:T(8,128)(2,1)S(1)}, f16[112,1792]{1,0:T(8,128)(2,1)S(1)}, u32[]{:S(2)}, u32[]{:S(2)}) %collective-permute-start.16) | collective-permute-done | bytes 401440 | tf_op jit(solution)/shard_map/ppermute | solution.py:18
  116.4 2.6 %fusion.22 = (f16[112,1792]{1,0:T(8,128)(2,1)}, f16[112,1792]{1,0:T(8,128)(2,1)}, f16[112,1792]{1,0:T(8,128)(2,1)}, f16[112,1792]{1,0:T(8,128)(2,1)}) fusion(f32[224,3584]{1,0:T(8,128)S(1)} %shard_map.43, f16[112,1792]{1,0:T(8,128)(2,1)S(1)} %collective-permute-done.10, f32[]{:T(128)} %bitcast.24, f32[]{:T(128)} %bitcast.23, ...), kind=kLoop, calls=%fused_computation.37 | loop fusion | flops 4014080 | bytes 6422536 | tf_op jit(solution)/shard_map/convert_element_type | solution.py:155
  119.0 3.2 %collective-permute-start.14 = (f16[112,1792]{1,0:T(8,128)(2,1)}, f16[112,1792]{1,0:T(8,128)(2,1)S(1)}, u32[]{:S(2)}, u32[]{:S(2)}) collective-permute-start(f16[112,1792]{1,0:T(8,128)(2,1)} %get-tuple-element.12), channel_id=1, source_target_pairs={{0,112},{16,0},{32,16},{48,32},{64,48},{80,64},{96,80},{112,96},{1... | collective-permute-start | bytes 1204232 | tf_op jit(solution)/shard_map/ppermute | solution.py:18
  122.3 3.2 %collective-permute-start.21 = (f16[112,1792]{1,0:T(8,128)(2,1)}, f16[112,1792]{1,0:T(8,128)(2,1)}, u32[]{:S(2)}, u32[]{:S(2)}) collective-permute-start(f16[112,1792]{1,0:T(8,128)(2,1)} %get-tuple-element.10), channel_id=1, source_target_pairs={{0,112},{16,0},{32,16},{48,32},{64,48},{80,64},{96,80},{112,96},{1... | collective-permute-start | bytes 1204232 | tf_op jit(solution)/shard_map/ppermute | solution.py:18
  125.7 4.6 %shard_map.42 = f32[112,3584]{1,0:T(8,128)S(1)} custom-call(bf16[112,1024]{1,0:T(8,128)(2,1)S(1)} %bitcast.46, bf16[1024,3584]{1,0:T(8,128)(2,1)} %get-tuple-element.7.scaled_ref), custom_call_target="tpu_custom_call" | custom-call | flops 822083584 | bytes 8945664 | tf_op jit(solution)/shard_map/pallas_call | solution.py:90
  130.3 2.4 %collective-permute-done.11 = f16[112,1792]{1,0:T(8,128)(2,1)S(1)} collective-permute-done((f16[112,1792]{1,0:T(8,128)(2,1)}, f16[112,1792]{1,0:T(8,128)(2,1)S(1)}, u32[]{:S(2)}, u32[]{:S(2)}) %collective-permute-start.11) | collective-permute-done | bytes 401440 | tf_op jit(solution)/shard_map/ppermute | solution.py:18
  132.7 4.5 %collective-permute-done.17 = f16[112,1792]{1,0:T(8,128)(2,1)S(1)} collective-permute-done((f16[112,1792]{1,0:T(8,128)(2,1)}, f16[112,1792]{1,0:T(8,128)(2,1)S(1)}, u32[]{:S(2)}, u32[]{:S(2)}) %collective-permute-start.17) | collective-permute-done | bytes 401440 | tf_op jit(solution)/shard_map/ppermute | solution.py:18
  (75 shorter events, 24.2 us)
Async XLA Ops:
  0.0 6.7 %copy-start = (bf16[1,1024,896]{2,1,0:T(8,128)(2,1)S(1)}, bf16[1,1024,896]{2,1,0:T(8,128)(2,1)}, u32[]{:S(2)}) copy-start(bf16[1,1024,896]{2,1,0:T(8,128)(2,1)} %param.5) | copy-start | bytes 5505028
  1.4 11.4 %collective-permute-start = (bf16[256,512]{1,0:T(8,128)(2,1)S(1)}, bf16[256,512]{1,0:T(8,128)(2,1)}, u32[]{:S(2)}, u32[]{:S(2)}) collective-permute-start(bf16[256,512]{1,0:T(8,128)(2,1)S(1)} %get-tuple-element.33.own_ref), channel_id=1, source_target_pairs={{128,0},{129,1},{130,2},{131,3},{132,4},{133,5},{134,6},{135,7},{1... | collective-permute-start | bytes 786440 | tf_op jit(solution)/shard_map/ppermute | solution.py:117
  2.7 15.5 %collective-permute-start.1 = (bf16[256,512]{1,0:T(8,128)(2,1)S(1)}, bf16[256,512]{1,0:T(8,128)(2,1)}, u32[]{:S(2)}, u32[]{:S(2)}) collective-permute-start(bf16[256,512]{1,0:T(8,128)(2,1)S(1)} %get-tuple-element.34.own_ref), channel_id=1, source_target_pairs={{128,0},{129,1},{130,2},{131,3},{132,4},{133,5},{134,6},{135,7},{1... | collective-permute-start | bytes 786440 | tf_op jit(solution)/shard_map/ppermute | solution.py:117
  4.0 19.7 %collective-permute-start.2 = (bf16[256,512]{1,0:T(8,128)(2,1)S(1)}, bf16[256,512]{1,0:T(8,128)(2,1)S(1)}, u32[]{:S(2)}, u32[]{:S(2)}) collective-permute-start(bf16[256,512]{1,0:T(8,128)(2,1)S(1)} %get-tuple-element.36.own_ref), channel_id=1, source_target_pairs={{128,0},{129,1},{130,2},{131,3},{132,4},{133,5},{134,6},{135,7},{1... | collective-permute-start | bytes 786440 | tf_op jit(solution)/shard_map/ppermute | solution.py:117
  5.3 22.9 %collective-permute-start.3 = (bf16[256,512]{1,0:T(8,128)(2,1)S(1)}, bf16[256,512]{1,0:T(8,128)(2,1)S(1)}, u32[]{:S(2)}, u32[]{:S(2)}) collective-permute-start(bf16[256,512]{1,0:T(8,128)(2,1)S(1)} %get-tuple-element.35.own_ref), channel_id=1, source_target_pairs={{128,0},{129,1},{130,2},{131,3},{132,4},{133,5},{134,6},{135,7},{1... | collective-permute-start | bytes 786440 | tf_op jit(solution)/shard_map/ppermute | solution.py:117
  8.8 4.0 %copy-start.1 = (s32[1,512]{1,0:T(1,128)S(1)}, s32[1,512]{1,0:T(1,128)}, u32[]{:S(2)}) copy-start(s32[1,512]{1,0:T(1,128)} %groups_ref.7) | copy-start | bytes 6148
  29.3 14.3 %all-to-all-start = ((f32[16,4,1024]{2,1,0:T(4,128)}), f32[16,4,1024]{2,1,0:T(4,128)S(1)}, u32[]{:S(2)}, u32[]{:S(2)}) async-start(f32[16,4,1024]{2,1,0:T(4,128)} %broadcast_in_dim.4), calls=%async_computation | async-start | bytes 524288 | tf_op jit(solution)/shard_map/all_to_all | solution.py:122
  45.0 12.9 %collective-permute-start.5 = (f32[8,128]{1,0:T(8,128)S(1)}, f32[8,128]{1,0:T(8,128)S(1)}, u32[]{:S(2)}, u32[]{:S(2)}) collective-permute-start(f32[8,128]{1,0:T(8,128)S(1)} %broadcast_in_dim.5), channel_id=1, source_target_pairs={{0,16},{16,32},{32,48},{48,64},{64,80},{80,96},{96,112},{112,0},{1... | collective-permute-start | bytes 12296 | tf_op jit(solution)/shard_map/ppermute | solution.py:18
  47.0 10.9 %collective-permute-start.6 = (f32[8,128]{1,0:T(8,128)S(1)}, f32[8,128]{1,0:T(8,128)S(1)}, u32[]{:S(2)}, u32[]{:S(2)}) collective-permute-start(f32[8,128]{1,0:T(8,128)S(1)} %broadcast_in_dim.5), channel_id=1, source_target_pairs={{0,112},{16,0},{32,16},{48,32},{64,48},{80,64},{96,80},{112,96},{1... | collective-permute-start | bytes 12296 | tf_op jit(solution)/shard_map/ppermute | solution.py:18
  55.8 16.0 %collective-permute-start.18 = (f16[112,1792]{1,0:T(8,128)(2,1)S(1)}, f16[112,1792]{1,0:T(8,128)(2,1)S(1)}, u32[]{:S(2)}, u32[]{:S(2)}) collective-permute-start(f16[112,1792]{1,0:T(8,128)(2,1)S(1)} %get-tuple-element.32), channel_id=1, source_target_pairs={{0,112},{16,0},{32,16},{48,32},{64,48},{80,64},{96,80},{112,96},{1... | collective-permute-start | bytes 1204232 | tf_op jit(solution)/shard_map/ppermute | solution.py:18
  57.8 14.0 %collective-permute-start.4 = (f16[112,1792]{1,0:T(8,128)(2,1)S(1)}, f16[112,1792]{1,0:T(8,128)(2,1)S(1)}, u32[]{:S(2)}, u32[]{:S(2)}) collective-permute-start(f16[112,1792]{1,0:T(8,128)(2,1)S(1)} %get-tuple-element.31), channel_id=1, source_target_pairs={{0,16},{16,32},{32,48},{48,64},{64,80},{80,96},{96,112},{112,0},{1... | collective-permute-start | bytes 1204232 | tf_op jit(solution)/shard_map/ppermute | solution.py:18
  57.9 12.7 %collective-permute-start.7 = (f32[8,128]{1,0:T(8,128)S(1)}, f32[8,128]{1,0:T(8,128)S(1)}, u32[]{:S(2)}, u32[]{:S(2)}) collective-permute-start(f32[8,128]{1,0:T(8,128)S(1)} %maximum_maximum_fusion.1), channel_id=1, source_target_pairs={{0,48},{16,64},{32,80},{48,96},{64,112},{80,0},{96,16},{112,32},{1... | collective-permute-start | bytes 12296 | tf_op jit(solution)/shard_map/ppermute | solution.py:18
  61.1 9.5 %collective-permute-start.8 = (f32[8,128]{1,0:T(8,128)S(1)}, f32[8,128]{1,0:T(8,128)S(1)}, u32[]{:S(2)}, u32[]{:S(2)}) collective-permute-start(f32[8,128]{1,0:T(8,128)S(1)} %maximum_maximum_fusion.1), channel_id=1, source_target_pairs={{0,80},{16,96},{32,112},{48,0},{64,16},{80,32},{96,48},{112,64},{1... | collective-permute-start | bytes 12296 | tf_op jit(solution)/shard_map/ppermute | solution.py:18
  71.9 6.4 %copy-start.6 = (bf16[1,1024,112]{2,1,0:T(8,128)(2,1)S(1)}, bf16[1,1024,112]{2,1,0:T(8,128)(2,1)}, u32[]{:S(2)}) copy-start(bf16[1,1024,112]{2,1,0:T(8,128)(2,1)} %get-tuple-element.23) | copy-start | bytes 688132
  71.9 6.5 %copy-start.5 = (bf16[1,1024,112]{2,1,0:T(8,128)(2,1)S(1)}, bf16[1,1024,112]{2,1,0:T(8,128)(2,1)}, u32[]{:S(2)}) copy-start(bf16[1,1024,112]{2,1,0:T(8,128)(2,1)} %get-tuple-element.22) | copy-start | bytes 688132
  73.1 12.4 %collective-permute-start.12 = (f16[112,1792]{1,0:T(8,128)(2,1)}, f16[112,1792]{1,0:T(8,128)(2,1)S(1)}, u32[]{:S(2)}, u32[]{:S(2)}) collective-permute-start(f16[112,1792]{1,0:T(8,128)(2,1)} %get-tuple-element.20), channel_id=1, source_target_pairs={{0,112},{16,0},{32,16},{48,32},{64,48},{80,64},{96,80},{112,96},{1... | collective-permute-start | bytes 1204232 | tf_op jit(solution)/shard_map/ppermute | solution.py:18
  75.0 13.4 %collective-permute-start.15 = (f16[112,1792]{1,0:T(8,128)(2,1)S(1)}, f16[112,1792]{1,0:T(8,128)(2,1)S(1)}, u32[]{:S(2)}, u32[]{:S(2)}) collective-permute-start(f16[112,1792]{1,0:T(8,128)(2,1)S(1)} %get-tuple-element.19), channel_id=1, source_target_pairs={{0,16},{16,32},{32,48},{48,64},{64,80},{80,96},{96,112},{112,0},{1... | collective-permute-start | bytes 1204232 | tf_op jit(solution)/shard_map/ppermute | solution.py:18
  75.1 17.4 %collective-permute-start.19 = (f16[112,1792]{1,0:T(8,128)(2,1)S(1)}, f16[112,1792]{1,0:T(8,128)(2,1)S(1)}, u32[]{:S(2)}, u32[]{:S(2)}) collective-permute-start(f16[112,1792]{1,0:T(8,128)(2,1)S(1)} %get-tuple-element.18), channel_id=1, source_target_pairs={{0,112},{16,0},{32,16},{48,32},{64,48},{80,64},{96,80},{112,96},{1... | collective-permute-start | bytes 1204232 | tf_op jit(solution)/shard_map/ppermute | solution.py:18
  78.3 16.7 %collective-permute-start.9 = (f16[112,1792]{1,0:T(8,128)(2,1)S(1)}, f16[112,1792]{1,0:T(8,128)(2,1)}, u32[]{:S(2)}, u32[]{:S(2)}) collective-permute-start(f16[112,1792]{1,0:T(8,128)(2,1)S(1)} %get-tuple-element.17), channel_id=1, source_target_pairs={{0,16},{16,32},{32,48},{48,64},{64,80},{80,96},{96,112},{112,0},{1... | collective-permute-start | bytes 1204232 | tf_op jit(solution)/shard_map/ppermute | solution.py:18
  94.9 8.9 %copy-start.4 = (bf16[1,1024,112]{2,1,0:T(8,128)(2,1)S(1)}, bf16[1,1024,112]{2,1,0:T(8,128)(2,1)}, u32[]{:S(2)}) copy-start(bf16[1,1024,112]{2,1,0:T(8,128)(2,1)} %get-tuple-element.25) | copy-start | bytes 688132
  95.0 9.0 %copy-start.3 = (bf16[1,1024,112]{2,1,0:T(8,128)(2,1)S(1)}, bf16[1,1024,112]{2,1,0:T(8,128)(2,1)}, u32[]{:S(2)}) copy-start(bf16[1,1024,112]{2,1,0:T(8,128)(2,1)} %get-tuple-element.24) | copy-start | bytes 688132
  97.3 13.6 %collective-permute-start.10 = (f16[112,1792]{1,0:T(8,128)(2,1)}, f16[112,1792]{1,0:T(8,128)(2,1)S(1)}, u32[]{:S(2)}, u32[]{:S(2)}) collective-permute-start(f16[112,1792]{1,0:T(8,128)(2,1)} %get-tuple-element.13), channel_id=1, source_target_pairs={{0,16},{16,32},{32,48},{48,64},{64,80},{80,96},{96,112},{112,0},{1... | collective-permute-start | bytes 1204232 | tf_op jit(solution)/shard_map/ppermute | solution.py:18
  97.3 13.6 %collective-permute-start.13 = (f16[112,1792]{1,0:T(8,128)(2,1)S(1)}, f16[112,1792]{1,0:T(8,128)(2,1)S(1)}, u32[]{:S(2)}, u32[]{:S(2)}) collective-permute-start(f16[112,1792]{1,0:T(8,128)(2,1)S(1)} %get-tuple-element.16), channel_id=1, source_target_pairs={{0,112},{16,0},{32,16},{48,32},{64,48},{80,64},{96,80},{112,96},{1... | collective-permute-start | bytes 1204232 | tf_op jit(solution)/shard_map/ppermute | solution.py:18
  100.6 15.9 %collective-permute-start.16 = (f16[112,1792]{1,0:T(8,128)(2,1)S(1)}, f16[112,1792]{1,0:T(8,128)(2,1)S(1)}, u32[]{:S(2)}, u32[]{:S(2)}) collective-permute-start(f16[112,1792]{1,0:T(8,128)(2,1)S(1)} %get-tuple-element.15), channel_id=1, source_target_pairs={{0,16},{16,32},{32,48},{48,64},{64,80},{80,96},{96,112},{112,0},{1... | collective-permute-start | bytes 1204232 | tf_op jit(solution)/shard_map/ppermute | solution.py:18
  100.6 15.9 %collective-permute-start.20 = (f16[112,1792]{1,0:T(8,128)(2,1)S(1)}, f16[112,1792]{1,0:T(8,128)(2,1)}, u32[]{:S(2)}, u32[]{:S(2)}) collective-permute-start(f16[112,1792]{1,0:T(8,128)(2,1)S(1)} %get-tuple-element.14), channel_id=1, source_target_pairs={{0,112},{16,0},{32,16},{48,32},{64,48},{80,64},{96,80},{112,96},{1... | collective-permute-start | bytes 1204232 | tf_op jit(solution)/shard_map/ppermute | solution.py:18
  109.4 16.1 %copy-start.2 = (bf16[1,1024,112]{2,1,0:T(8,128)(2,1)S(1)}, bf16[1,1024,112]{2,1,0:T(8,128)(2,1)}, u32[]{:S(2)}) copy-start(bf16[1,1024,112]{2,1,0:T(8,128)(2,1)} %get-tuple-element.27) | copy-start | bytes 688132
  119.0 13.6 %collective-permute-start.11 = (f16[112,1792]{1,0:T(8,128)(2,1)}, f16[112,1792]{1,0:T(8,128)(2,1)S(1)}, u32[]{:S(2)}, u32[]{:S(2)}) collective-permute-start(f16[112,1792]{1,0:T(8,128)(2,1)} %get-tuple-element.9), channel_id=1, source_target_pairs={{0,16},{16,32},{32,48},{48,64},{64,80},{80,96},{96,112},{112,0},{1... | collective-permute-start | bytes 1204232 | tf_op jit(solution)/shard_map/ppermute | solution.py:18
  119.0 13.6 %collective-permute-start.14 = (f16[112,1792]{1,0:T(8,128)(2,1)}, f16[112,1792]{1,0:T(8,128)(2,1)S(1)}, u32[]{:S(2)}, u32[]{:S(2)}) collective-permute-start(f16[112,1792]{1,0:T(8,128)(2,1)} %get-tuple-element.12), channel_id=1, source_target_pairs={{0,112},{16,0},{32,16},{48,32},{64,48},{80,64},{96,80},{112,96},{1... | collective-permute-start | bytes 1204232 | tf_op jit(solution)/shard_map/ppermute | solution.py:18
  122.3 14.9 %collective-permute-start.17 = (f16[112,1792]{1,0:T(8,128)(2,1)}, f16[112,1792]{1,0:T(8,128)(2,1)S(1)}, u32[]{:S(2)}, u32[]{:S(2)}) collective-permute-start(f16[112,1792]{1,0:T(8,128)(2,1)} %get-tuple-element.11), channel_id=1, source_target_pairs={{0,16},{16,32},{32,48},{48,64},{64,80},{80,96},{96,112},{112,0},{1... | collective-permute-start | bytes 1204232 | tf_op jit(solution)/shard_map/ppermute | solution.py:18
  122.3 15.7 %collective-permute-start.21 = (f16[112,1792]{1,0:T(8,128)(2,1)}, f16[112,1792]{1,0:T(8,128)(2,1)}, u32[]{:S(2)}, u32[]{:S(2)}) collective-permute-start(f16[112,1792]{1,0:T(8,128)(2,1)} %get-tuple-element.10), channel_id=1, source_target_pairs={{0,112},{16,0},{32,16},{48,32},{64,48},{80,64},{96,80},{112,96},{1... | collective-permute-start | bytes 1204232 | tf_op jit(solution)/shard_map/ppermute | solution.py:18
  137.2 0.7 copy-start.7

commit v2 on v0

v2 whole, which is shorter than its diff:
```python
import functools

import jax
import jax.numpy as jnp
from jax import lax
from jax.experimental import pallas as pl
from jax.experimental.pallas import tpu as pltpu
from jax.sharding import PartitionSpec as P

D = 8192
GROUPS = 4
DP = 8
LANES = 128
SENT = jnp.float16
VMEM_LIMIT = 48 * 1024 * 1024
KEPT = (384, 256)


def shift(value, axis, steps):
    count = lax.axis_size(axis)
    return lax.ppermute(value, axis, [(i, (i + steps) % count) for i in range(count)])


def square_kernel(groups_ref, own_ref, *refs):
    group = lax.broadcasted_iota(jnp.int32, (16, groups_ref.shape[1]), 0)
    onehot = jnp.where(groups_ref[...] == group, 1.0, 0.0).astype(jnp.bfloat16)
    total = own_ref[...].astype(jnp.float32)
    if len(refs) == 2:
        total = total + refs[0][...].astype(jnp.float32)
    rest = total * total
    result = jnp.zeros((16, own_ref.shape[0]), jnp.float32)
    for _ in range(3):
        part = rest.astype(jnp.bfloat16)
        rest = rest - part.astype(jnp.float32)
        result += lax.dot_general(
            onehot, part, (((1,), (1,)), ((), ())), preferred_element_type=jnp.float32
        )
    refs[-1][...] = result[:GROUPS]


def group_squares(groups, *parts):
    return pl.pallas_call(
        square_kernel,
        out_shape=jax.ShapeDtypeStruct((GROUPS, parts[0].shape[0]), jnp.float32),
        compiler_params=pltpu.CompilerParams(vmem_limit_bytes=VMEM_LIMIT),
    )(groups, *parts)


def section_weights(own, groups):
    tokens = own.shape[0]
    keep = sum(KEPT)
    pieces, start = [], 0
    for size in KEPT:
        pieces.append(own[start : start + size])
        start += size
    moved = own[keep:]
    first_groups = lax.ppermute(groups, "section", [(0, 1)])
    first = lax.ppermute(moved, "section", [(0, 1)])
    later = [lax.ppermute(piece, "section", [(1, 0)]) for piece in pieces]
    alone = group_squares(groups, moved)
    back = lax.ppermute(group_squares(first_groups, moved, first), "section", [(1, 0)])
    partial = [group_squares(groups, piece, other) for piece, other in zip(pieces, later)]
    partial.append(jnp.where(lax.axis_index("section") == 0, back, alone))
    partial = jnp.concatenate(partial, 1)
    count = lax.axis_size("tensor")
    partial += lax.ppermute(partial, "tensor", [(i, i ^ 1) for i in range(count)])
    chips = [list(range(core, count, 2)) for core in (0, 1)]
    spread = jnp.broadcast_to(partial[None], (count // 2, GROUPS, tokens))
    spread = lax.all_to_all(spread, "tensor", 0, 0, axis_index_groups=chips, tiled=True)
    return spread.sum(0) / D


def product_kernel(order, me_ref, weight_ref, turned_ref, *refs):
    rows_ref = refs[-1]
    outs = refs[:-1]
    group = pl.program_id(0)
    me = me_ref[0]
    count = outs[-1].shape[2]
    low = group < GROUPS // 2

    @pl.when(group % (GROUPS // 2) == 0)
    def _():
        for n, (first, second, _) in enumerate(order):
            at = lax.rem(me + jnp.where(low, first, second), DP) * count
            rows_ref[n * count : (n + 1) * count, :] = turned_ref[
                pl.ds(pl.multiple_of(at, 16), count), :
            ]

    weight = weight_ref[pl.ds(group, 1), :]
    scaled = (turned_ref[...].astype(jnp.float32) * weight).astype(jnp.bfloat16)
    result = lax.dot_general(
        rows_ref[...], scaled, (((1,), (1,)), ((), ())), preferred_element_type=jnp.float32
    )
    for n in range(len(order)):
        for c in range(outs[n].shape[1]):
            outs[n][0, c] = result[n * count : (n + 1) * count, c * LANES : (c + 1) * LANES]


def products(me, weight, turned, *order):
    width, tokens = turned.shape
    count = width // DP
    tiles = width // LANES
    half = GROUPS // 2 * tiles
    block = (1, tiles, count, LANES)
    split = pl.BlockSpec(block, lambda g, me: (g // 2, g % 2, 0, 0))
    swapped = pl.BlockSpec(block, lambda g, me: (1 - g // 2, g % 2, 0, 0))
    return pl.pallas_call(
        functools.partial(product_kernel, order),
        grid_spec=pltpu.PrefetchScalarGridSpec(
            num_scalar_prefetch=1,
            grid=(GROUPS,),
            in_specs=[
                pl.BlockSpec((GROUPS, tokens), lambda g, me: (0, 0)),
                pl.BlockSpec((width, tokens), lambda g, me: (0, 0)),
            ],
            out_specs=[swapped if first > second else split for first, second, _ in order],
            scratch_shapes=[pltpu.VMEM((len(order) * count, tokens), jnp.bfloat16)],
        ),
        out_shape=[
            jax.ShapeDtypeStruct((2, half + room, count, LANES), jnp.float32)
            for _, _, room in order
        ],
        compiler_params=pltpu.CompilerParams(vmem_limit_bytes=VMEM_LIMIT),
        cost_estimate=pl.CostEstimate(flops=1, bytes_accessed=1, transcendentals=0),
    )(me, weight, turned)


def add_kernel(left_ref, right_ref, out_ref):
    out_ref[...] = left_ref[...] + right_ref[...]


def add(left, right):
    block = pl.BlockSpec((1, *left.shape[1:]), lambda i: (i, 0, 0, 0))
    return pl.pallas_call(
        add_kernel,
        grid=(left.shape[0],),
        in_specs=[block, block],
        out_specs=block,
        out_shape=jax.ShapeDtypeStruct(left.shape, left.dtype),
        compiler_params=pltpu.CompilerParams(vmem_limit_bytes=VMEM_LIMIT),
        cost_estimate=pl.CostEstimate(flops=8_000_000_000, bytes_accessed=1, transcendentals=0),
    )(left, right)


def on_device(grads, groups, acts):
    me = lax.axis_index("dp").astype(jnp.int32).reshape(1)
    weight = section_weights(grads[0], groups)

    cols = acts[0]
    tokens, width = cols.shape
    rows = width // DP
    half = GROUPS // 2 * width // LANES
    turned = cols.T
    peak = jnp.max(jnp.abs(turned), axis=0).astype(jnp.float32)

    top = jnp.max(weight * (peak * peak)[None])
    top = jnp.ceil(jnp.log2(jnp.maximum(top, 1e-30)))
    top = lax.optimization_barrier(jnp.broadcast_to(top, (1, LANES)))
    far, early3 = products(me, weight, turned, (4, 4, 1), (5, 3, 0))

    bits = {k: 15 - (tokens * k - 1).bit_length() for k in (1, 2, 3, 4)}
    room = lax.broadcasted_iota(jnp.int32, (half + 1, rows, LANES), 0) == half

    def pack(value, level, count):
        value = value * jnp.exp2(bits[count] - level)[None]
        if value.shape[0] > half:
            value = jnp.where(room, level[None], value)
        return value.astype(SENT)

    def unpack(value, level, count):
        return value.astype(jnp.float32) * jnp.exp2(level - bits[count])[None]

    def tag_of(value):
        return value[half].astype(jnp.float32)

    way = (1, -1)
    both = (0, 1)

    def send(packed):
        return [shift(packed[i], "dp", way[i]) for i in both]

    odd = send([pack(far[i], top, 1) for i in both])
    packed = [pack(early3[i], top, 1) for i in both]
    even = send(packed)
    weight = lax.optimization_barrier((weight, *packed))[0]
    mine, late3, early2, late2, early1, late1 = rest = products(
        me, weight, turned, (0, 0, 0), (3, 5, 1), (6, 2, 0), (2, 6, 1), (7, 1, 0), (1, 7, 1)
    )
    odd = lax.optimization_barrier((*odd, *rest))[:2]
    for count, early, late in ((2, early2, late3), (3, early1, late2), (4, None, late1)):
        level = [tag_of(odd[i]) for i in both]
        after = [jnp.maximum(top, level[i]) for i in both]
        packed = [
            pack(late[i] + unpack(odd[i], level[i], count - 1), after[i], count) for i in both
        ]
        odd = send(packed)
        if early is not None:
            packed = [
                pack(early[i] + unpack(even[i], level[i], count - 1), after[i], count)
                for i in both
            ]
            even = send(packed)
            odd = lax.optimization_barrier((*odd, *packed))[:2]
    last = [tag_of(odd[i]) for i in both]

    factor = 1.0 / (tokens * DP)
    even = [unpack(even[i], level[i], 3) for i in both]
    odd = [unpack(odd[i][:half], last[i], 4) for i in both]
    total = add(mine, jnp.stack(even[::-1])) + jnp.stack(odd)
    total = jnp.transpose(total, (2, 0, 1, 3)) * factor
    return total.reshape(1, rows, GROUPS * width)


def solution(mesh):
    return jax.shard_map(
        on_device,
        mesh=mesh,
        in_specs=(
            P("section", "dp", "tensor"),
            P("section", "tensor"),
            P("section", "dp", "tensor"),
        ),
        out_specs=P("section", ("tensor", "dp"), None),
        check_vma=False,
    )
```

time: 292 us -> 119 us (0.41)
  waiting for transfers between devices: 157 us -> 44.9 us
  blocking collectives: 63.4 us -> 0 us
  starting transfers between devices: 5.17 us -> 41.6 us
  local copies, waits for them, and re-layouts: 24.4 us -> 7.73 us
  Pallas kernels: 0 us -> 15.8 us
  matrix products: 14.5 us -> 0 us
  between operations: 13.5 us -> 1.01 us
  other arithmetic: 12.2 us -> 5.52 us
    unnamed x2 -> x0, waiting for transfers between devices: 140 us -> none
    psum x1 -> x0, blocking collectives: 63.4 us -> none  [on_device(): summed_list.append(lax.psum(partial_value, 'tensor'))]
    ppermute x4 -> x20, starting transfers between devices: 5.17 us -> 34.2 us  [the longest x14 21.1 us: shift(): lax.ppermute(value, axis, [(i, (i + steps) % count) for i in range(count)])]
    ppermute x4 -> x20, waiting for transfers between devices: 16.7 us -> 38.3 us  [the longest x14 36 us: shift(): lax.ppermute(value, axis, [(i, (i + steps) % count) for i in range(count)])]
    unnamed x9, local copies, waits for them, and re-layouts: 20.1 us -> 2.93 us
    pallas_call x0 -> x7, Pallas kernels: none -> 15.8 us  [the longest x2 13.7 us: products(): pl.pallas_call(functools.partial(product_kernel, order), grid_spec=pltpu....]
    dot_general x5 -> x0, matrix products: 14.5 us -> none  [the longest x1 12.7 us: contract_tokens(): lax.dot_general(left, right, (((0,), (0,)), ((), ())), preferred_element_...]
    all_to_all x0 -> x1, starting transfers between devices: none -> 7.38 us  [section_weights(): lax.all_to_all(spread, 'tensor', 0, 0, axis_index_groups=chips, tiled=True)]
  transfers between devices with their start and end apart: 5 -> 21, of which waited for: 5 -> 14; matrix products, arithmetic and copies ran while one was open for 2% -> 7% of each run, Pallas kernels for 0% -> 10%
where the time goes in v2:
time: 119 us; the launch traced here: 116 us
  waiting for transfers between devices  44.9 us (38%)
  starting transfers between devices  41.6 us (35%)
  Pallas kernels  15.8 us (13%)
  local copies, waits for them, and re-layouts  7.73 us (6%)
  other arithmetic  5.52 us (5%)
    ppermute x14, waiting for transfers between devices, shift(): lax.ppermute(value, axis, [(i, (i + steps) % count) for i in range(count)])  36 us
    ppermute x14, starting transfers between devices, shift(): lax.ppermute(value, axis, [(i, (i + steps) % count) for i in range(count)])  21.1 us
    pallas_call x2, Pallas kernels, products(): pl.pallas_call(functools.partial(product_kernel, order), grid_spec=pltpu....  13.7 us
    all_to_all x1, starting transfers between devices, section_weights(): lax.all_to_all(spread, 'tensor', 0, 0, axis_index_groups=chips, tiled=True)  7.38 us
    all_to_all x1, waiting for transfers between devices, section_weights(): lax.all_to_all(spread, 'tensor', 0, 0, axis_index_groups=chips, tiled=True)  6.56 us
    ppermute x1, starting transfers between devices, section_weights(): first = lax.ppermute(moved, 'section', [(0, 1)])  4.59 us
    ppermute x1, starting transfers between devices, section_weights(): first_groups = lax.ppermute(groups, 'section', [(0, 1)])  4.56 us
    convert_element_type x7, other arithmetic, pack(): return value.astype(SENT)  3.84 us
  transfers between devices with their start and end apart: 21, of which 14 were waited for; matrix products, arithmetic and copies ran while one was open for 7% of the time, Pallas kernels for 10%

profile of v2, /device:TPU:8, one launch (start us, length us, event | category | flops | bytes accessed | tf_op | source)
XLA Modules:
  0.0 116.5 jit_solution(17654084992291133919)
XLA Ops:
  0.0 1.2 %slice_bitcast_fusion.1 = (bf16[384,512]{1,0:T(8,128)(2,1)S(1)}, bf16[384,512]{1,0:T(8,128)(2,1)S(1)}) fusion(bf16[1,1024,512]{2,1,0:T(8,128)(2,1)} %param.3), kind=kLoop, calls=%fused_computation.56 | loop fusion | bytes 1572864 | tf_op jit(solution)/shard_map/slice | solution.py:54
  1.2 1.3 %collective-permute-start = (bf16[384,512]{1,0:T(8,128)(2,1)S(1)}, bf16[384,512]{1,0:T(8,128)(2,1)S(1)}, u32[]{:S(2)}, u32[]{:S(2)}) collective-permute-start(bf16[384,512]{1,0:T(8,128)(2,1)S(1)} %get-tuple-element.49.own_ref), channel_id=1, source_target_pairs={{128,0},{129,1},{130,2},{131,3},{132,4},{133,5},{134,6},{135,7},{1... | collective-permute-start | bytes 1179656 | tf_op jit(solution)/shard_map/ppermute | solution.py:59
  2.5 4.6 %collective-permute-start.3 = (bf16[384,512]{1,0:T(8,128)(2,1)S(1)}, bf16[384,512]{1,0:T(8,128)(2,1)S(1)}, u32[]{:S(2)}, u32[]{:S(2)}) collective-permute-start(bf16[384,512]{1,0:T(8,128)(2,1)S(1)} %get-tuple-element.50.own_ref), channel_id=1, source_target_pairs={{0,128},{1,129},{2,130},{3,131},{4,132},{5,133},{6,134},{7,135},{8... | collective-permute-start | bytes 1179656 | tf_op jit(solution)/shard_map/ppermute | solution.py:58
  8.1 1.3 %collective-permute-start.1 = (bf16[256,512]{1,0:T(8,128)(2,1)S(1)}, bf16[256,512]{1,0:T(8,128)(2,1)S(1)}, u32[]{:S(2)}, u32[]{:S(2)}) collective-permute-start(bf16[256,512]{1,0:T(8,128)(2,1)S(1)} %slice_bitcast_fusion.2.own_ref), channel_id=1, source_target_pairs={{128,0},{129,1},{130,2},{131,3},{132,4},{133,5},{134,6},{135,7},{1... | collective-permute-start | bytes 786440 | tf_op jit(solution)/shard_map/ppermute | solution.py:59
  9.4 4.6 %collective-permute-start.2 = (s32[1,512]{1,0:T(1,128)S(1)}, s32[1,512]{1,0:T(1,128)S(1)}, u32[]{:S(2)}, u32[]{:S(2)}) collective-permute-start(s32[1,512]{1,0:T(1,128)S(1)} %copy-done.1), channel_id=1, source_target_pairs={{0,128},{1,129},{2,130},{3,131},{4,132},{5,133},{6,134},{7,135},{8... | collective-permute-start | bytes 6152 | tf_op jit(solution)/shard_map/ppermute | solution.py:57
  13.9 1.3 %collective-permute-done.2.groups_ref = s32[1,512]{1,0:T(1,128)S(1)} collective-permute-done((s32[1,512]{1,0:T(1,128)S(1)}, s32[1,512]{1,0:T(1,128)S(1)}, u32[]{:S(2)}, u32[]{:S(2)}) %collective-permute-start.2) | collective-permute-done | bytes 2080 | tf_op jit(solution)/shard_map/ppermute | solution.py:57
  15.7 1.3 %collective-permute-start.4 = (f32[4,384]{1,0:T(4,128)S(1)}, f32[4,384]{1,0:T(4,128)S(1)}, u32[]{:S(2)}, u32[]{:S(2)}) collective-permute-start(f32[4,384]{1,0:T(4,128)S(1)} %shard_map.39), channel_id=1, source_target_pairs={{128,0},{129,1},{130,2},{131,3},{132,4},{133,5},{134,6},{135,7},{1... | collective-permute-start | bytes 18440 | tf_op jit(solution)/shard_map/ppermute | solution.py:61
  17.5 2.9 %copy.10 = bf16[1,1024,896]{1,2,0:T(8,128)(2,1)S(1)} copy(bf16[1,1024,896]{2,1,0:T(8,128)(2,1)} %param.5) | data formatting | bytes 3670016 | tf_op args[2]
  23.4 7.4 %all-to-all-start = ((f32[8,4,1024]{2,1,0:T(4,128)}), f32[8,4,1024]{2,1,0:T(4,128)S(1)}, u32[]{:S(2)}, u32[]{:S(2)}) async-start(f32[8,4,1024]{2,1,0:T(4,128)} %broadcast_in_dim.104), calls=%async_computation | async-start | bytes 262144 | tf_op jit(solution)/shard_map/all_to_all | solution.py:69
  30.7 6.6 %all-to-all-done = f32[8,4,1024]{2,1,0:T(4,128)S(1)} async-done(((f32[8,4,1024]{2,1,0:T(4,128)}), f32[8,4,1024]{2,1,0:T(4,128)S(1)}, u32[]{:S(2)}, u32[]{:S(2)}) %all-to-all-start) | async-done | bytes 131104 | tf_op jit(solution)/shard_map/all_to_all | solution.py:69
  38.7 4.2 %shard_map.41 = (f32[2,15,112,128]{3,2,1,0:T(8,128)S(1)}, f32[2,14,112,128]{3,2,1,0:T(8,128)S(1)}) custom-call(s32[1]{0:T(128)} %bitcast.me_ref, f32[4,1024]{1,0:T(4,128)S(1)} %get-tuple-element.21.weight_ref, bf16[896,1024]{1,0:T(8,128)(2,1)S(1)} %bitcast.156), custom_call_target="tpu_custom_call" | custom-call | flops 1 | bytes 1 | tf_op jit(solution)/shard_map/pallas_call | solution.py:107
  43.2 5.9 %collective-permute-start.8 = (f16[15,112,128]{2,1,0:T(8,128)(2,1)S(1)}, f16[15,112,128]{2,1,0:T(8,128)(2,1)S(1)}, u32[]{:S(2)}, u32[]{:S(2)}) collective-permute-start(f16[15,112,128]{2,1,0:T(8,128)(2,1)S(1)} %get-tuple-element.35), channel_id=1, source_target_pairs={{0,112},{16,0},{32,16},{48,32},{64,48},{80,64},{96,80},{112,96},{1... | collective-permute-start | bytes 1290248 | tf_op jit(solution)/shard_map/ppermute | solution.py:21
  49.3 3.3 %collective-permute-start.6 = (f16[14,112,128]{2,1,0:T(8,128)(2,1)S(1)}, f16[14,112,128]{2,1,0:T(8,128)(2,1)S(1)}, u32[]{:S(2)}, u32[]{:S(2)}) collective-permute-start(f16[14,112,128]{2,1,0:T(8,128)(2,1)S(1)} %get-tuple-element.43), channel_id=1, source_target_pairs={{0,112},{16,0},{32,16},{48,32},{64,48},{80,64},{96,80},{112,96},{1... | collective-permute-start | bytes 1204232 | tf_op jit(solution)/shard_map/ppermute | solution.py:21
  52.6 9.5 %shard_map.42 = (f32[2,14,112,128]{3,2,1,0:T(8,128)S(1)}, f32[2,15,112,128]{3,2,1,0:T(8,128)}, f32[2,14,112,128]{3,2,1,0:T(8,128)S(1)}, f32[2,15,112,128]{3,2,1,...) custom-call(s32[1]{0:T(128)} %bitcast.me_ref, f32[4,1024]{1,0:T(4,128)S(1)} %get-tuple-element.21.weight_ref, ...), custom_call_target="tpu_custom_call" | custom-call | flops 1 | bytes 1 | tf_op jit(solution)/shard_map/pallas_call | solution.py:107
  62.1 1.1 collective-permute-done.7
  63.2 1.9 %fusion.16 = (f16[15,112,128]{2,1,0:T(8,128)(2,1)S(1)}, f16[15,112,128]{2,1,0:T(8,128)(2,1)S(1)}) fusion(f16[15,112,128]{2,1,0:T(8,128)(2,1)S(1)} %collective-permute-done.8, f32[2,15,112,128]{3,2,1,0:T(8,128)} %get-tuple-element.26, f32[112,128]{1,0:T(8,128)S(1)} %get-tuple-element.60, f32[112,128]{1,0:T(8,128)S(1)} %get-tuple-element.67, ...), kind=kLoop, calls=%fused_computation.24 | loop fusion | flops 2580480 | bytes 3784719 | tf_op jit(solution)/shard_map/convert_element_type | solution.py:168
  65.1 2.2 %collective-permute-start.11 = (f16[15,112,128]{2,1,0:T(8,128)(2,1)S(1)}, f16[15,112,128]{2,1,0:T(8,128)(2,1)S(1)}, u32[]{:S(2)}, u32[]{:S(2)}) collective-permute-start(f16[15,112,128]{2,1,0:T(8,128)(2,1)S(1)} %get-tuple-element.41), channel_id=1, source_target_pairs={{0,112},{16,0},{32,16},{48,32},{64,48},{80,64},{96,80},{112,96},{1... | collective-permute-start | bytes 1290248 | tf_op jit(solution)/shard_map/ppermute | solution.py:21
  67.3 2.5 %collective-permute-done.12 = f16[14,112,128]{2,1,0:T(8,128)(2,1)S(1)} collective-permute-done((f16[14,112,128]{2,1,0:T(8,128)(2,1)S(1)}, f16[14,112,128]{2,1,0:T(8,128)(2,1)S(1)}, u32[]{:S(2)}, u32[]{:S(2)}) %collective-permute-start.12) | collective-permute-done | bytes 401440 | tf_op jit(solution)/shard_map/ppermute | solution.py:21
  71.0 1.3 %collective-permute-start.16 = (f16[14,112,128]{2,1,0:T(8,128)(2,1)S(1)}, f16[14,112,128]{2,1,0:T(8,128)(2,1)S(1)}, u32[]{:S(2)}, u32[]{:S(2)}) collective-permute-start(f16[14,112,128]{2,1,0:T(8,128)(2,1)S(1)} %get-tuple-element.48), channel_id=1, source_target_pairs={{0,16},{16,32},{32,48},{48,64},{64,80},{80,96},{96,112},{112,0},{1... | collective-permute-start | bytes 1204232 | tf_op jit(solution)/shard_map/ppermute | solution.py:21
  72.3 5.5 %collective-permute-done.11 = f16[15,112,128]{2,1,0:T(8,128)(2,1)S(1)} collective-permute-done((f16[15,112,128]{2,1,0:T(8,128)(2,1)S(1)}, f16[15,112,128]{2,1,0:T(8,128)(2,1)S(1)}, u32[]{:S(2)}, u32[]{:S(2)}) %collective-permute-start.11) | collective-permute-done | bytes 430112 | tf_op jit(solution)/shard_map/ppermute | solution.py:21
  77.8 3.5 %collective-permute-done.10 = f16[15,112,128]{2,1,0:T(8,128)(2,1)S(1)} collective-permute-done((f16[15,112,128]{2,1,0:T(8,128)(2,1)S(1)}, f16[15,112,128]{2,1,0:T(8,128)(2,1)S(1)}, u32[]{:S(2)}, u32[]{:S(2)}) %collective-permute-start.10) | collective-permute-done | bytes 430112 | tf_op jit(solution)/shard_map/ppermute | solution.py:21
  82.0 2.0 %collective-permute-start.14 = (f16[15,112,128]{2,1,0:T(8,128)(2,1)S(1)}, f16[15,112,128]{2,1,0:T(8,128)(2,1)S(1)}, u32[]{:S(2)}, u32[]{:S(2)}) collective-permute-start(f16[15,112,128]{2,1,0:T(8,128)(2,1)S(1)} %get-tuple-element.40), channel_id=1, source_target_pairs={{0,16},{16,32},{32,48},{48,64},{64,80},{80,96},{96,112},{112,0},{1... | collective-permute-start | bytes 1290248 | tf_op jit(solution)/shard_map/ppermute | solution.py:21
  84.0 2.3 %collective-permute-done.9 = f16[14,112,128]{2,1,0:T(8,128)(2,1)S(1)} collective-permute-done((f16[14,112,128]{2,1,0:T(8,128)(2,1)S(1)}, f16[14,112,128]{2,1,0:T(8,128)(2,1)S(1)}, u32[]{:S(2)}, u32[]{:S(2)}) %collective-permute-start.9) | collective-permute-done | bytes 401440 | tf_op jit(solution)/shard_map/ppermute | solution.py:21
  86.3 3.7 %collective-permute-done.16 = f16[14,112,128]{2,1,0:T(8,128)(2,1)S(1)} collective-permute-done((f16[14,112,128]{2,1,0:T(8,128)(2,1)S(1)}, f16[14,112,128]{2,1,0:T(8,128)(2,1)S(1)}, u32[]{:S(2)}, u32[]{:S(2)}) %collective-permute-start.16) | collective-permute-done | bytes 401440 | tf_op jit(solution)/shard_map/ppermute | solution.py:21
  90.4 2.0 %collective-permute-start.17 = (f16[14,112,128]{2,1,0:T(8,128)(2,1)S(1)}, f16[14,112,128]{2,1,0:T(8,128)(2,1)S(1)}, u32[]{:S(2)}, u32[]{:S(2)}) collective-permute-start(f16[14,112,128]{2,1,0:T(8,128)(2,1)S(1)} %get-tuple-element.46), channel_id=1, source_target_pairs={{0,16},{16,32},{32,48},{48,64},{64,80},{80,96},{96,112},{112,0},{1... | collective-permute-start | bytes 1204232 | tf_op jit(solution)/shard_map/ppermute | solution.py:21
  92.4 3.1 %collective-permute-done.15 = f16[15,112,128]{2,1,0:T(8,128)(2,1)S(1)} collective-permute-done((f16[15,112,128]{2,1,0:T(8,128)(2,1)S(1)}, f16[15,112,128]{2,1,0:T(8,128)(2,1)S(1)}, u32[]{:S(2)}, u32[]{:S(2)}) %collective-permute-start.15) | collective-permute-done | bytes 430112 | tf_op jit(solution)/shard_map/ppermute | solution.py:21
  95.5 3.7 %collective-permute-done.14 = f16[15,112,128]{2,1,0:T(8,128)(2,1)S(1)} collective-permute-done((f16[15,112,128]{2,1,0:T(8,128)(2,1)S(1)}, f16[15,112,128]{2,1,0:T(8,128)(2,1)S(1)}, u32[]{:S(2)}, u32[]{:S(2)}) %collective-permute-start.14) | collective-permute-done | bytes 430112 | tf_op jit(solution)/shard_map/ppermute | solution.py:21
  99.8 3.2 %collective-permute-start.19 = (f16[15,112,128]{2,1,0:T(8,128)(2,1)S(1)}, f16[15,112,128]{2,1,0:T(8,128)(2,1)S(1)}, u32[]{:S(2)}, u32[]{:S(2)}) collective-permute-start(f16[15,112,128]{2,1,0:T(8,128)(2,1)S(1)} %get-tuple-element.38), channel_id=1, source_target_pairs={{0,112},{16,0},{32,16},{48,32},{64,48},{80,64},{96,80},{112,96},{1... | collective-permute-start | bytes 1290248 | tf_op jit(solution)/shard_map/ppermute | solution.py:21
  103.0 1.1 collective-permute-done.13
  104.2 3.6 %collective-permute-done.17 = f16[14,112,128]{2,1,0:T(8,128)(2,1)S(1)} collective-permute-done((f16[14,112,128]{2,1,0:T(8,128)(2,1)S(1)}, f16[14,112,128]{2,1,0:T(8,128)(2,1)S(1)}, u32[]{:S(2)}, u32[]{:S(2)}) %collective-permute-start.17) | collective-permute-done | bytes 401440 | tf_op jit(solution)/shard_map/ppermute | solution.py:21
  108.2 5.9 %collective-permute-done.18 = f16[15,112,128]{2,1,0:T(8,128)(2,1)S(1)} collective-permute-done((f16[15,112,128]{2,1,0:T(8,128)(2,1)S(1)}, f16[15,112,128]{2,1,0:T(8,128)(2,1)S(1)}, u32[]{:S(2)}, u32[]{:S(2)}) %collective-permute-start.18) | collective-permute-done | bytes 430112 | tf_op jit(solution)/shard_map/ppermute | solution.py:21
  115.0 1.4 %reshape.89 = f32[1,112,3584]{2,1,0:T(8,128)} reshape(f32[112,2,14,128]{3,2,1,0:T(8,128)S(1)} %copy.11) | data formatting | bytes 3211264 | tf_op jit(solution)/shard_map/reshape | solution.py:211
  (59 shorter events, 10.0 us)
Async XLA Ops:
  0.0 9.4 %copy-start.1 = (s32[1,512]{1,0:T(1,128)S(1)}, s32[1,512]{1,0:T(1,128)}, u32[]{:S(2)}) copy-start(s32[1,512]{1,0:T(1,128)} %groups_ref.5) | copy-start | bytes 6148
  1.2 19.6 %collective-permute-start = (bf16[384,512]{1,0:T(8,128)(2,1)S(1)}, bf16[384,512]{1,0:T(8,128)(2,1)S(1)}, u32[]{:S(2)}, u32[]{:S(2)}) collective-permute-start(bf16[384,512]{1,0:T(8,128)(2,1)S(1)} %get-tuple-element.49.own_ref), channel_id=1, source_target_pairs={{128,0},{129,1},{130,2},{131,3},{132,4},{133,5},{134,6},{135,7},{1... | collective-permute-start | bytes 1179656 | tf_op jit(solution)/shard_map/ppermute | solution.py:59
  2.5 12.7 %collective-permute-start.3 = (bf16[384,512]{1,0:T(8,128)(2,1)S(1)}, bf16[384,512]{1,0:T(8,128)(2,1)S(1)}, u32[]{:S(2)}, u32[]{:S(2)}) collective-permute-start(bf16[384,512]{1,0:T(8,128)(2,1)S(1)} %get-tuple-element.50.own_ref), channel_id=1, source_target_pairs={{0,128},{1,129},{2,130},{3,131},{4,132},{5,133},{6,134},{7,135},{8... | collective-permute-start | bytes 1179656 | tf_op jit(solution)/shard_map/ppermute | solution.py:58
  8.1 12.4 %collective-permute-start.1 = (bf16[256,512]{1,0:T(8,128)(2,1)S(1)}, bf16[256,512]{1,0:T(8,128)(2,1)S(1)}, u32[]{:S(2)}, u32[]{:S(2)}) collective-permute-start(bf16[256,512]{1,0:T(8,128)(2,1)S(1)} %slice_bitcast_fusion.2.own_ref), channel_id=1, source_target_pairs={{128,0},{129,1},{130,2},{131,3},{132,4},{133,5},{134,6},{135,7},{1... | collective-permute-start | bytes 786440 | tf_op jit(solution)/shard_map/ppermute | solution.py:59
  9.4 5.9 %collective-permute-start.2 = (s32[1,512]{1,0:T(1,128)S(1)}, s32[1,512]{1,0:T(1,128)S(1)}, u32[]{:S(2)}, u32[]{:S(2)}) collective-permute-start(s32[1,512]{1,0:T(1,128)S(1)} %copy-done.1), channel_id=1, source_target_pairs={{0,128},{1,129},{2,130},{3,131},{4,132},{5,133},{6,134},{7,135},{8... | collective-permute-start | bytes 6152 | tf_op jit(solution)/shard_map/ppermute | solution.py:57
  15.7 5.6 %collective-permute-start.4 = (f32[4,384]{1,0:T(4,128)S(1)}, f32[4,384]{1,0:T(4,128)S(1)}, u32[]{:S(2)}, u32[]{:S(2)}) collective-permute-start(f32[4,384]{1,0:T(4,128)S(1)} %shard_map.39), channel_id=1, source_target_pairs={{128,0},{129,1},{130,2},{131,3},{132,4},{133,5},{134,6},{135,7},{1... | collective-permute-start | bytes 18440 | tf_op jit(solution)/shard_map/ppermute | solution.py:61
  20.4 18.2 %copy-start = (bf16[1,1024,896]{1,2,0:T(8,128)(2,1)}, bf16[1,1024,896]{1,2,0:T(8,128)(2,1)S(1)}, u32[]{:S(2)}) copy-start(bf16[1,1024,896]{1,2,0:T(8,128)(2,1)S(1)} %copy.10) | copy-start | bytes 5505028
  21.4 1.3 %collective-permute-start.5 = (f32[4,1024]{1,0:T(4,128)S(1)}, f32[4,1024]{1,0:T(4,128)S(1)}, u32[]{:S(2)}, u32[]{:S(2)}) collective-permute-start(f32[4,1024]{1,0:T(4,128)S(1)} %pad_maximum_fusion.1), channel_id=1, source_target_pairs={{0,1},{1,0},{2,3},{3,2},{4,5},{5,4},{6,7},{7,6},{8,9},{9,8},{10,11... | collective-permute-start | bytes 49160 | tf_op jit(solution)/shard_map/ppermute | solution.py:66
  23.4 13.9 %all-to-all-start = ((f32[8,4,1024]{2,1,0:T(4,128)}), f32[8,4,1024]{2,1,0:T(4,128)S(1)}, u32[]{:S(2)}, u32[]{:S(2)}) async-start(f32[8,4,1024]{2,1,0:T(4,128)} %broadcast_in_dim.104), calls=%async_computation | async-start | bytes 262144 | tf_op jit(solution)/shard_map/all_to_all | solution.py:69
  43.2 18.9 %collective-permute-start.8 = (f16[15,112,128]{2,1,0:T(8,128)(2,1)S(1)}, f16[15,112,128]{2,1,0:T(8,128)(2,1)S(1)}, u32[]{:S(2)}, u32[]{:S(2)}) collective-permute-start(f16[15,112,128]{2,1,0:T(8,128)(2,1)S(1)} %get-tuple-element.35), channel_id=1, source_target_pairs={{0,112},{16,0},{32,16},{48,32},{64,48},{80,64},{96,80},{112,96},{1... | collective-permute-start | bytes 1290248 | tf_op jit(solution)/shard_map/ppermute | solution.py:21
  49.1 14.1 %collective-permute-start.7 = (f16[15,112,128]{2,1,0:T(8,128)(2,1)S(1)}, f16[15,112,128]{2,1,0:T(8,128)(2,1)S(1)}, u32[]{:S(2)}, u32[]{:S(2)}) collective-permute-start(f16[15,112,128]{2,1,0:T(8,128)(2,1)S(1)} %get-tuple-element.36), channel_id=1, source_target_pairs={{0,16},{16,32},{32,48},{48,64},{64,80},{80,96},{96,112},{112,0},{1... | collective-permute-start | bytes 1290248 | tf_op jit(solution)/shard_map/ppermute | solution.py:21
  49.3 18.0 %collective-permute-start.6 = (f16[14,112,128]{2,1,0:T(8,128)(2,1)S(1)}, f16[14,112,128]{2,1,0:T(8,128)(2,1)S(1)}, u32[]{:S(2)}, u32[]{:S(2)}) collective-permute-start(f16[14,112,128]{2,1,0:T(8,128)(2,1)S(1)} %get-tuple-element.43), channel_id=1, source_target_pairs={{0,112},{16,0},{32,16},{48,32},{64,48},{80,64},{96,80},{112,96},{1... | collective-permute-start | bytes 1204232 | tf_op jit(solution)/shard_map/ppermute | solution.py:21
  52.6 17.3 %collective-permute-start.12 = (f16[14,112,128]{2,1,0:T(8,128)(2,1)S(1)}, f16[14,112,128]{2,1,0:T(8,128)(2,1)S(1)}, u32[]{:S(2)}, u32[]{:S(2)}) collective-permute-start(f16[14,112,128]{2,1,0:T(8,128)(2,1)S(1)} %get-tuple-element.44), channel_id=1, source_target_pairs={{0,16},{16,32},{32,48},{48,64},{64,80},{80,96},{96,112},{112,0},{1... | collective-permute-start | bytes 1204232 | tf_op jit(solution)/shard_map/ppermute | solution.py:21
  65.1 12.7 %collective-permute-start.11 = (f16[15,112,128]{2,1,0:T(8,128)(2,1)S(1)}, f16[15,112,128]{2,1,0:T(8,128)(2,1)S(1)}, u32[]{:S(2)}, u32[]{:S(2)}) collective-permute-start(f16[15,112,128]{2,1,0:T(8,128)(2,1)S(1)} %get-tuple-element.41), channel_id=1, source_target_pairs={{0,112},{16,0},{32,16},{48,32},{64,48},{80,64},{96,80},{112,96},{1... | collective-permute-start | bytes 1290248 | tf_op jit(solution)/shard_map/ppermute | solution.py:21
  67.3 14.1 %copy-start.3 = (f32[2,15,112,128]{3,2,1,0:T(8,128)S(1)}, f32[2,15,112,128]{3,2,1,0:T(8,128)}, u32[]{:S(2)}) copy-start(f32[2,15,112,128]{3,2,1,0:T(8,128)} %get-tuple-element.27) | copy-start | bytes 5160964
  67.3 14.1 %collective-permute-start.10 = (f16[15,112,128]{2,1,0:T(8,128)(2,1)S(1)}, f16[15,112,128]{2,1,0:T(8,128)(2,1)S(1)}, u32[]{:S(2)}, u32[]{:S(2)}) collective-permute-start(f16[15,112,128]{2,1,0:T(8,128)(2,1)S(1)} %get-tuple-element.42), channel_id=1, source_target_pairs={{0,16},{16,32},{32,48},{48,64},{64,80},{80,96},{96,112},{112,0},{1... | collective-permute-start | bytes 1290248 | tf_op jit(solution)/shard_map/ppermute | solution.py:21
  70.2 16.1 %collective-permute-start.9 = (f16[14,112,128]{2,1,0:T(8,128)(2,1)S(1)}, f16[14,112,128]{2,1,0:T(8,128)(2,1)S(1)}, u32[]{:S(2)}, u32[]{:S(2)}) collective-permute-start(f16[14,112,128]{2,1,0:T(8,128)(2,1)S(1)} %get-tuple-element.47), channel_id=1, source_target_pairs={{0,112},{16,0},{32,16},{48,32},{64,48},{80,64},{96,80},{112,96},{1... | collective-permute-start | bytes 1204232 | tf_op jit(solution)/shard_map/ppermute | solution.py:21
  71.0 19.0 %collective-permute-start.16 = (f16[14,112,128]{2,1,0:T(8,128)(2,1)S(1)}, f16[14,112,128]{2,1,0:T(8,128)(2,1)S(1)}, u32[]{:S(2)}, u32[]{:S(2)}) collective-permute-start(f16[14,112,128]{2,1,0:T(8,128)(2,1)S(1)} %get-tuple-element.48), channel_id=1, source_target_pairs={{0,16},{16,32},{32,48},{48,64},{64,80},{80,96},{96,112},{112,0},{1... | collective-permute-start | bytes 1204232 | tf_op jit(solution)/shard_map/ppermute | solution.py:21
  81.9 13.6 %collective-permute-start.15 = (f16[15,112,128]{2,1,0:T(8,128)(2,1)S(1)}, f16[15,112,128]{2,1,0:T(8,128)(2,1)S(1)}, u32[]{:S(2)}, u32[]{:S(2)}) collective-permute-start(f16[15,112,128]{2,1,0:T(8,128)(2,1)S(1)} %get-tuple-element.39), channel_id=1, source_target_pairs={{0,112},{16,0},{32,16},{48,32},{64,48},{80,64},{96,80},{112,96},{1... | collective-permute-start | bytes 1290248 | tf_op jit(solution)/shard_map/ppermute | solution.py:21
  82.0 17.3 %copy-start.2 = (f32[2,15,112,128]{3,2,1,0:T(8,128)S(1)}, f32[2,15,112,128]{3,2,1,0:T(8,128)}, u32[]{:S(2)}) copy-start(f32[2,15,112,128]{3,2,1,0:T(8,128)} %get-tuple-element.28) | copy-start | bytes 5160964
  82.0 17.2 %collective-permute-start.14 = (f16[15,112,128]{2,1,0:T(8,128)(2,1)S(1)}, f16[15,112,128]{2,1,0:T(8,128)(2,1)S(1)}, u32[]{:S(2)}, u32[]{:S(2)}) collective-permute-start(f16[15,112,128]{2,1,0:T(8,128)(2,1)S(1)} %get-tuple-element.40), channel_id=1, source_target_pairs={{0,16},{16,32},{32,48},{48,64},{64,80},{80,96},{96,112},{112,0},{1... | collective-permute-start | bytes 1290248 | tf_op jit(solution)/shard_map/ppermute | solution.py:21
  90.3 13.8 %collective-permute-start.13 = (f16[14,112,128]{2,1,0:T(8,128)(2,1)S(1)}, f16[14,112,128]{2,1,0:T(8,128)(2,1)S(1)}, u32[]{:S(2)}, u32[]{:S(2)}) collective-permute-start(f16[14,112,128]{2,1,0:T(8,128)(2,1)S(1)} %get-tuple-element.45), channel_id=1, source_target_pairs={{0,112},{16,0},{32,16},{48,32},{64,48},{80,64},{96,80},{112,96},{1... | collective-permute-start | bytes 1204232 | tf_op jit(solution)/shard_map/ppermute | solution.py:21
  90.4 17.4 %collective-permute-start.17 = (f16[14,112,128]{2,1,0:T(8,128)(2,1)S(1)}, f16[14,112,128]{2,1,0:T(8,128)(2,1)S(1)}, u32[]{:S(2)}, u32[]{:S(2)}) collective-permute-start(f16[14,112,128]{2,1,0:T(8,128)(2,1)S(1)} %get-tuple-element.46), channel_id=1, source_target_pairs={{0,16},{16,32},{32,48},{48,64},{64,80},{80,96},{96,112},{112,0},{1... | collective-permute-start | bytes 1204232 | tf_op jit(solution)/shard_map/ppermute | solution.py:21
  99.7 14.3 %collective-permute-start.18 = (f16[15,112,128]{2,1,0:T(8,128)(2,1)S(1)}, f16[15,112,128]{2,1,0:T(8,128)(2,1)S(1)}, u32[]{:S(2)}, u32[]{:S(2)}) collective-permute-start(f16[15,112,128]{2,1,0:T(8,128)(2,1)S(1)} %get-tuple-element.37), channel_id=1, source_target_pairs={{0,16},{16,32},{32,48},{48,64},{64,80},{80,96},{96,112},{112,0},{1... | collective-permute-start | bytes 1290248 | tf_op jit(solution)/shard_map/ppermute | solution.py:21
  99.8 14.3 %collective-permute-start.19 = (f16[15,112,128]{2,1,0:T(8,128)(2,1)S(1)}, f16[15,112,128]{2,1,0:T(8,128)(2,1)S(1)}, u32[]{:S(2)}, u32[]{:S(2)}) collective-permute-start(f16[15,112,128]{2,1,0:T(8,128)(2,1)S(1)} %get-tuple-element.38), channel_id=1, source_target_pairs={{0,112},{16,0},{32,16},{48,32},{64,48},{80,64},{96,80},{112,96},{1... | collective-permute-start | bytes 1290248 | tf_op jit(solution)/shard_map/ppermute | solution.py:21
